TPU v7x, 256 devices: a whole 4x4x8 slice. The times are simulated.
256 devices in a mesh: dp: 8 (over x, core), vocab: 32 (over z, y).
Axes of the slice: x: 4, y: 4, z: 8, core: 2. Of those that a mesh axis runs over, the one named last changes fastest.
Arguments:
- encoder_rows: bfloat16 [64, 32, 1536], P(None, 'dp', 'vocab'), may hold values from -6 to 6
- predictor_rows: bfloat16 [64, 129, 640], P('dp'), may hold values from -6 to 6
- enc_weight: bfloat16 [1536, 640], P('dp'), may hold values from -0.15625 to 0.15625
- pred_weight: bfloat16 [640, 640], P('dp'), may hold values from -0.25 to 0.25
- out_weight: bfloat16 [640, 4096], P(None, 'vocab'), may hold values from -48 to 48
- frame_lengths: int32 [64], P('dp'), may hold values from 16 to 32
- label_lengths: int32 [64], P('dp'), may hold values from 32 to 128
- label_ids: int32 [64, 128], P('dp'), may hold values from 1 to 4095
Outputs:
- losses: float32 [64], P('dp')
All inputs are finite; a program needn't handle non-finite values.
Results may differ from a plain program's by a relative error of at most 0.00035.
Values may be sent and summed in bfloat16 or wider, within the bound.
A program may use at most 128 MiB of HBM per device.

v0:
```python
import jax
import jax.numpy as jnp
from jax import lax
from jax.sharding import PartitionSpec as P

neg_floor = -1e30


def combine(earlier, later):
    return (earlier[0] + later[0], jnp.logaddexp(later[1], later[0] + earlier[1]))


def lattice(blank_lp, label_lp, frame_lengths, label_lengths):
    batch_rows, frames, positions = blank_lp.shape
    u_iota = jnp.arange(positions)
    start_row = jnp.where(
        u_iota[None, :] == 0,
        jnp.zeros((batch_rows, positions), jnp.float32),
        jnp.full((batch_rows, positions), neg_floor, jnp.float32),
    )

    def advance(state, inputs):
        incoming, result = state
        blank_t, label_t, frame_index = inputs
        gains = jnp.concatenate([jnp.zeros((batch_rows, 1), jnp.float32), label_t[:, :-1]], axis=1)
        unused, alpha_t = lax.associative_scan(combine, (gains, incoming), axis=1)
        ending = alpha_t + blank_t
        here = jnp.sum(
            jnp.where(u_iota[None, :] == label_lengths[:, None], ending, jnp.zeros_like(ending)),
            axis=1,
        )
        result = jnp.where(frame_index == frame_lengths - 1, here, result)
        return ((ending, result), None)

    inputs = (jnp.moveaxis(blank_lp, 1, 0), jnp.moveaxis(label_lp, 1, 0), jnp.arange(frames))
    (unused, result), unused_out = lax.scan(
        advance, (start_row, jnp.zeros((batch_rows,), jnp.float32)), inputs
    )
    return -result / (frame_lengths + label_lengths).astype(jnp.float32)


def shards(
    encoder_rows,
    predictor_rows,
    enc_weight,
    pred_weight,
    out_weight,
    frame_lengths,
    label_lengths,
    label_ids,
):
    full_enc_w, full_pred_w = (
        lax.all_gather(enc_weight, "dp", axis=0, tiled=True),
        lax.all_gather(pred_weight, "dp", axis=0, tiled=True),
    )
    joint_width = full_enc_w.shape[1]
    relaid = lax.all_to_all(encoder_rows, "dp", split_axis=0, concat_axis=1, tiled=True)
    shard_piece = lax.all_gather(relaid, "vocab", axis=2, tiled=True)
    enc_sum = jnp.dot(
        shard_piece.reshape(-1, shard_piece.shape[2]),
        full_enc_w,
        preferred_element_type=jnp.float32,
    )
    enc_proj = enc_sum.astype(jnp.bfloat16).reshape(relaid.shape[0], relaid.shape[1], joint_width)
    utt_count, frames = (enc_proj.shape[0], enc_proj.shape[1])
    positions = predictor_rows.shape[1]
    pred_proj = (
        jnp.dot(
            predictor_rows.reshape(-1, predictor_rows.shape[2]),
            full_pred_w,
            preferred_element_type=jnp.float32,
        )
        .astype(jnp.bfloat16)
        .reshape(utt_count, positions, joint_width)
    )
    vocab_cols = out_weight.shape[1]
    vocab_start = lax.axis_index("vocab") * vocab_cols
    padded_labels = jnp.concatenate([label_ids, jnp.zeros((utt_count, 1), jnp.int32)], axis=1)
    row_ids = jnp.broadcast_to(padded_labels[:, None, :], (utt_count, 8, positions)).reshape(-1)
    local_col = row_ids - vocab_start
    owned_col = (local_col >= 0) & (local_col < vocab_cols)
    clipped = jnp.clip(local_col, 0, vocab_cols - 1)
    blank_owned = vocab_start == 0
    block_shape = (utt_count, 8, positions)
    enc_wide = enc_proj.astype(jnp.float32)
    pred_wide = pred_proj.astype(jnp.float32)

    def block_logits(block_index):
        enc_block = lax.dynamic_slice_in_dim(enc_wide, block_index * 8, 8, 1)
        hidden = (
            jnp.tanh(enc_block[:, :, None, :] + pred_wide[:, None, :, :])
            .astype(jnp.bfloat16)
            .reshape(-1, joint_width)
        )
        logits = jnp.dot(hidden, out_weight, preferred_element_type=jnp.float32)
        local_max = jnp.max(logits, axis=1)
        picked = jnp.take_along_axis(logits, clipped[:, None], axis=1)[:, 0]
        label_part = jnp.where(owned_col, picked, jnp.zeros_like(picked))
        blank_part = jnp.where(blank_owned, logits[:, 0], jnp.zeros_like(picked))
        return (logits, local_max, label_part, blank_part)

    def one_block(unused, block_index):
        logits, local_max, label_part, blank_part = block_logits(block_index)
        maxima = lax.pmax(local_max.astype(jnp.bfloat16), "vocab").astype(local_max.dtype)
        local_sum = jnp.sum(jnp.exp(logits - maxima[:, None]), axis=1)
        totals, label_val, blank_val = (
            lax.psum(local_sum.astype(jnp.bfloat16), "vocab").astype(jnp.float32),
            lax.psum(label_part.astype(jnp.bfloat16), "vocab").astype(jnp.float32),
            lax.psum(blank_part.astype(jnp.bfloat16), "vocab").astype(jnp.float32),
        )
        log_norm = maxima + jnp.log(totals)
        return (
            unused,
            (
                (blank_val - log_norm).reshape(block_shape),
                (label_val - log_norm).reshape(block_shape),
            ),
        )

    unused, (blank_blocks, label_blocks) = lax.scan(
        one_block, jnp.zeros((), jnp.float32), jnp.arange(frames // 8)
    )
    blank_lp = jnp.moveaxis(blank_blocks, 0, 1).reshape(utt_count, frames, positions)
    label_lp = jnp.moveaxis(label_blocks, 0, 1).reshape(utt_count, frames, positions)
    return lattice(blank_lp, label_lp, frame_lengths, label_lengths)


def solution(mesh):
    return jax.shard_map(
        shards,
        mesh=mesh,
        in_specs=(
            P(None, "dp", "vocab"),
            P("dp", None, None),
            P("dp", None),
            P("dp", None),
            P(None, "vocab"),
            P("dp"),
            P("dp"),
            P("dp", None),
        ),
        out_specs=P("dp"),
        check_vma=False,
    )
```

profile of v0, /device:TPU:2, one launch (start us, length us, event | category | flops | bytes accessed | tf_op | source)
XLA Modules:
  0.0 1961.0 jit_solution(16304269980369078835)
XLA Ops:
  16.4 13.9 all_gather.11
  35.7 61.3 %all_gather.9 = bf16[8,32,1536]{1,0,2:T(8,128)(2,1)} all-gather(bf16[8,32,48]{1,0,2:T(8,128)(2,1)S(1)} %copy.47), channel_id=1, replica_groups=mesh['dp'=8,'vocab'=32] {'vocab'}, dimensions={2}, use_global_device_ids=true | all-gather | bytes 811008 | tf_op jit(solution)/shard_map/all_gather | solution.py:58
  105.2 1729.7 %while.28 = (s32[]{:T(128)}, f32[4,8,8,129]{3,2,1,0:T(8,128)S(1)}, f32[4,8,8,129]{3,2,1,0:T(8,128)}, pred[]{:T(512)}, s32[4]{0:T(128)S(1)}, /*index=5*/f32[8,32,...) while((s32[]{:T(128)}, f32[4,8,8,129]{3,2,1,0:T(8,128)S(1)}, ...), condition=%wide.region_7.8_spmd.clone, body=%wide.region_0.7_spmd.clone.sunk | while | flops 1366640640 | bytes 55528552 | solution.py:120
  114.5 11.4 convert_element_type.105
  125.9 8.9 fusion.45
  134.7 140.4 %pmax.9 = bf16[8256]{0:T(1024)(128)(2,1)S(1)} all-reduce(bf16[8256]{0:T(1024)(128)(2,1)S(1)} %get-tuple-element.425), channel_id=1, replica_groups=mesh['dp'=8,'vocab'=32] {'vocab'}, use_global_device_ids=true, to_apply=%region_3.3 | all-reduce | flops 8256 | bytes 33024 | tf_op jit(solution)/shard_map/while/body/eval_jaxpr/pmax | solution.py:104
  282.1 113.8 %gather_fusion = bf16[8256]{0:T(1024)(128)(2,1)S(1)} fusion(f32[8256,128]{1,0:T(8,128)} %get-tuple-element.424, s32[8256]{0:T(1024)S(1)} %fusion.47), kind=kCustom, calls=%fused_computation.clone.clone.1 | custom fusion | bytes 99072 | tf_op jit(solution)/shard_map/while/body/eval_jaxpr/jit(take_along_axis)/gather | solution.py:97
  400.8 137.8 %all-reduce.18 = (bf16[8256]{0:T(1024)(128)(2,1)S(1)}, bf16[8256]{0:T(1024)(128)(2,1)S(1)}, bf16[8256]{0:T(1024)(128)(2,1)S(1)}) all-reduce(bf16[8256]{0:T(1024)(128)(2,1)S(1)} %fusion.46, bf16[8256]{0:T(1024)(128)(2,1)S(1)} %exponential_reduce_fusion.2, ...), channel_id=1, replica_groups=mesh['dp'=8,'vocab'=32] {'vocab'}, use_global_device_ids=true, to_apply=%region_1.1 | all-reduce | flops 24768 | bytes 99072 | tf_op jit(solution)/shard_map/while/body/eval_jaxpr/psum | solution.py:109
  548.9 11.4 convert_element_type.105
  560.3 8.9 fusion.45
  569.1 137.7 %pmax.9 = bf16[8256]{0:T(1024)(128)(2,1)S(1)} all-reduce(bf16[8256]{0:T(1024)(128)(2,1)S(1)} %get-tuple-element.425), channel_id=1, replica_groups=mesh['dp'=8,'vocab'=32] {'vocab'}, use_global_device_ids=true, to_apply=%region_3.3 | all-reduce | flops 8256 | bytes 33024 | tf_op jit(solution)/shard_map/while/body/eval_jaxpr/pmax | solution.py:104
  713.9 113.8 %gather_fusion = bf16[8256]{0:T(1024)(128)(2,1)S(1)} fusion(f32[8256,128]{1,0:T(8,128)} %get-tuple-element.424, s32[8256]{0:T(1024)S(1)} %fusion.47), kind=kCustom, calls=%fused_computation.clone.clone.1 | custom fusion | bytes 99072 | tf_op jit(solution)/shard_map/while/body/eval_jaxpr/jit(take_along_axis)/gather | solution.py:97
  832.5 137.7 %all-reduce.18 = (bf16[8256]{0:T(1024)(128)(2,1)S(1)}, bf16[8256]{0:T(1024)(128)(2,1)S(1)}, bf16[8256]{0:T(1024)(128)(2,1)S(1)}) all-reduce(bf16[8256]{0:T(1024)(128)(2,1)S(1)} %fusion.46, bf16[8256]{0:T(1024)(128)(2,1)S(1)} %exponential_reduce_fusion.2, ...), channel_id=1, replica_groups=mesh['dp'=8,'vocab'=32] {'vocab'}, use_global_device_ids=true, to_apply=%region_1.1 | all-reduce | flops 24768 | bytes 99072 | tf_op jit(solution)/shard_map/while/body/eval_jaxpr/psum | solution.py:109
  980.6 11.4 convert_element_type.105
  992.0 8.9 fusion.45
  1000.9 137.7 %pmax.9 = bf16[8256]{0:T(1024)(128)(2,1)S(1)} all-reduce(bf16[8256]{0:T(1024)(128)(2,1)S(1)} %get-tuple-element.425), channel_id=1, replica_groups=mesh['dp'=8,'vocab'=32] {'vocab'}, use_global_device_ids=true, to_apply=%region_3.3 | all-reduce | flops 8256 | bytes 33024 | tf_op jit(solution)/shard_map/while/body/eval_jaxpr/pmax | solution.py:104
  1145.6 113.8 %gather_fusion = bf16[8256]{0:T(1024)(128)(2,1)S(1)} fusion(f32[8256,128]{1,0:T(8,128)} %get-tuple-element.424, s32[8256]{0:T(1024)S(1)} %fusion.47), kind=kCustom, calls=%fused_computation.clone.clone.1 | custom fusion | bytes 99072 | tf_op jit(solution)/shard_map/while/body/eval_jaxpr/jit(take_along_axis)/gather | solution.py:97
  1264.3 137.7 %all-reduce.18 = (bf16[8256]{0:T(1024)(128)(2,1)S(1)}, bf16[8256]{0:T(1024)(128)(2,1)S(1)}, bf16[8256]{0:T(1024)(128)(2,1)S(1)}) all-reduce(bf16[8256]{0:T(1024)(128)(2,1)S(1)} %fusion.46, bf16[8256]{0:T(1024)(128)(2,1)S(1)} %exponential_reduce_fusion.2, ...), channel_id=1, replica_groups=mesh['dp'=8,'vocab'=32] {'vocab'}, use_global_device_ids=true, to_apply=%region_1.1 | all-reduce | flops 24768 | bytes 99072 | tf_op jit(solution)/shard_map/while/body/eval_jaxpr/psum | solution.py:109
  1412.4 11.4 convert_element_type.105
  1423.8 8.9 fusion.45
  1432.6 137.7 %pmax.9 = bf16[8256]{0:T(1024)(128)(2,1)S(1)} all-reduce(bf16[8256]{0:T(1024)(128)(2,1)S(1)} %get-tuple-element.425), channel_id=1, replica_groups=mesh['dp'=8,'vocab'=32] {'vocab'}, use_global_device_ids=true, to_apply=%region_3.3 | all-reduce | flops 8256 | bytes 33024 | tf_op jit(solution)/shard_map/while/body/eval_jaxpr/pmax | solution.py:104
  1577.4 113.8 %gather_fusion = bf16[8256]{0:T(1024)(128)(2,1)S(1)} fusion(f32[8256,128]{1,0:T(8,128)} %get-tuple-element.424, s32[8256]{0:T(1024)S(1)} %fusion.47), kind=kCustom, calls=%fused_computation.clone.clone.1 | custom fusion | bytes 99072 | tf_op jit(solution)/shard_map/while/body/eval_jaxpr/jit(take_along_axis)/gather | solution.py:97
  1696.0 137.7 %all-reduce.18 = (bf16[8256]{0:T(1024)(128)(2,1)S(1)}, bf16[8256]{0:T(1024)(128)(2,1)S(1)}, bf16[8256]{0:T(1024)(128)(2,1)S(1)}) all-reduce(bf16[8256]{0:T(1024)(128)(2,1)S(1)} %fusion.46, bf16[8256]{0:T(1024)(128)(2,1)S(1)} %exponential_reduce_fusion.2, ...), channel_id=1, replica_groups=mesh['dp'=8,'vocab'=32] {'vocab'}, use_global_device_ids=true, to_apply=%region_1.1 | all-reduce | flops 24768 | bytes 99072 | tf_op jit(solution)/shard_map/while/body/eval_jaxpr/psum | solution.py:109
  1838.6 115.0 %while.29 = (s32[]{:T(128)}, f32[8,129]{0,1:T(8,128)S(1)}, f32[8]{0:T(128)S(1)}, f32[32,8,129]{1,2,0:T(8,128)}, f32[32,8,129]{1,2,0:T(8,128)S(1)}, /*index=5*/s3...) while((s32[]{:T(128)}, f32[8,129]{0,1:T(8,128)S(1)}, ...), condition=%wide.region_10.11_spmd.clone, body=%wide.region_8.10_spmd.clone.sunk | while | flops 26443 | bytes 173283 | solution.py:36
  (2712 shorter events, 218.9 us)
Async XLA Ops:
  6.5 9.8 copy-start.4
  6.5 9.8 copy-start.1
  6.5 95.2 %all-gather.2.cloned.1.call-start = ((), (), s32[]{:S(2)}) async-start(), calls=%async_computation.1 | async-start | bytes 2211840 | tf_op jit(solution)/shard_map/all_gather | solution.py:53
  8.9 26.4 %all-to-all-start = ((bf16[8,2,768]{2,1,0:T(2,128)(2,1)}), bf16[8,2,768]{2,1,0:T(2,128)(2,1)S(1)}, u32[]{:S(2)}, u32[]{:S(2)}) async-start(bf16[8,2,768]{2,1,0:T(2,128)(2,1)} %reshape.112), calls=%async_computation | async-start | bytes 49152 | tf_op jit(solution)/shard_map/all_to_all | solution.py:57
  97.0 8.2 copy-start
  1834.8 3.7 copy-start.2
  1834.8 3.8 copy-start.3
Sparse Core Ops, SparseCore 0:
  9.2 29.9 all-gather.1
where the time goes:
time: 1980 us; the launch traced here: 1960 us
  blocking collectives  1180 us (60%)
  local copies, waits for them, and re-layouts  599 us (30%)
  other arithmetic  109 us (6%)
  matrix products  41 us (2%)
    pmax x4, blocking collectives, one_block(): lax.pmax(local_max.astype(jnp.bfloat16), 'vocab').astype(local_max.dtype)  554 us
    psum x4, blocking collectives, one_block(): lax.psum(blank_part.astype(jnp.bfloat16), 'vocab').astype(jnp.float32)  551 us
    gather x4, local copies, waits for them, and re-layouts, block_logits(): picked = jnp.take_along_axis(logits, clipped[:, None], axis=1)[:, 0]  455 us
    all_gather x1, blocking collectives, shards(): shard_piece = lax.all_gather(relaid, 'vocab', axis=2, tiled=True)  61.3 us
    convert_element_type x4, local copies, waits for them, and re-layouts, block_logits(): hidden = jnp.tanh(enc_block[:, :, None, :] + pred_wide[:, None, :, :]).as...  45.6 us
  transfers between devices with their start and end apart: 2, of which 0 were waited for; matrix products, arithmetic and copies ran while one was open for 1% of the time, Pallas kernels for 0%

commit v1 on v0

v1 whole, which is shorter than its diff:
```python
import functools

import jax
import jax.numpy as jnp
from jax import lax
from jax.experimental import pallas as pl
from jax.experimental.pallas import tpu as pltpu
from jax.sharding import PartitionSpec as P

MESH = pl.DeviceIdType.MESH
NY = 4
NEG = -1e30
NT = (((1,), (1,)), ((), ()))


def joint_kernel(
    ndp,
    nv,
    xin,
    prows,
    wenc,
    wpred,
    wout,
    flen,
    llen,
    labels,
    out,
    bufb,
    xp,
    bufx,
    we,
    wp,
    prow,
    part,
    enc,
    pred,
    wt,
    wlab,
    hid,
    stat,
    lp,
    lossbuf,
    state0,
    prow_sem,
    xd_s,
    xd_r,
    xz_s,
    xz_r,
    we_s,
    we_r,
    wp_s,
    wp_r,
    ring_s,
    ring_r,
    sib_s,
    sib_r,
    y_s,
    y_r,
    st_s,
    st_r,
    lo_s,
    lo_r,
):
    nz = nv // NY
    nx = ndp // 2
    i = lax.axis_index("dp")
    v = lax.axis_index("vocab")
    z = v // NY
    y = v % NY
    x = i // 2
    c = i % 2
    sib = 2 * x + (1 - c)
    frames = part.shape[1]
    width = part.shape[2]
    feat = xin.shape[2]
    quarter = frames // ndp

    def vz(s):
        return ((z + s + nz) % nz) * NY + y

    def vy(s):
        return z * NY + (y + s) % NY

    barrier = pltpu.get_barrier_semaphore()
    for s in range(1, ndp):
        pl.semaphore_signal(barrier, inc=1, device_id=((i + s) % ndp, v), device_id_type=MESH)
    for s in range(1, nz):
        pl.semaphore_signal(barrier, inc=1, device_id=(i, vz(s)), device_id_type=MESH)
    for s in range(1, NY):
        pl.semaphore_signal(barrier, inc=1, device_id=(i, vy(s)), device_id_type=MESH)

    prow_copy = pltpu.make_async_copy(prows.at[z], prow, prow_sem)
    prow_copy.start()

    bufb[i] = xin[i]
    own_wt = wout[...].astype(jnp.float32).T.astype(jnp.bfloat16)
    wt[z] = own_wt
    erow = pl.multiple_of(48 * y, 16)
    we[i] = wenc[pl.ds(erow, feat), :]
    wp[i] = wpred[...]
    stat[y, 2] = jnp.zeros(stat.shape[2:], jnp.float32)

    pl.semaphore_wait(barrier, (ndp - 1) + (nz - 1) + (NY - 1))

    def remote(src, dst, ssem, rsem, dev):
        return pltpu.make_async_remote_copy(
            src_ref=src, dst_ref=dst, send_sem=ssem, recv_sem=rsem, device_id=dev, device_id_type=MESH
        )

    sends = []

    def go(cp):
        cp.start()
        sends.append(cp)
        return cp

    xd = []
    for s in range(1, ndp):
        k = (i + s) % ndp
        xd.append(go(remote(xin.at[k], bufb.at[i], xd_s.at[s - 1], xd_r.at[s - 1], (k, v))))

    half = wt.shape[1] // 2
    my_half = pl.ds(pl.multiple_of(c * half, half), half)

    def ring_copy(origin, s, direction):
        idx = s - 1 if direction > 0 else nz // 2 + s - 1
        blk = wt.at[origin, my_half]
        return remote(blk, blk, ring_s.at[idx], ring_r.at[idx], (i, vz(direction)))

    def sib_copy(origin, idx):
        blk = wt.at[origin, my_half]
        return remote(blk, blk, sib_s.at[idx], sib_r.at[idx], (sib, v))

    n_right, n_left = nz // 2, nz - 1 - nz // 2
    rights = [go(ring_copy(z, 1, 1))]
    lefts = [go(ring_copy(z, 1, -1))]
    sibs = []

    we_c, wp_c = [], []
    for s in range(1, nx):
        dev = (2 * ((x + s) % nx) + c, v)
        we_c.append(go(remote(we.at[i], we.at[i], we_s.at[s - 1], we_r.at[s - 1], dev)))
    we_sib = [go(remote(we.at[i], we.at[i], we_s.at[nx - 1], we_r.at[nx - 1], (sib, v)))]
    for s in range(1, nx):
        dev = (2 * ((x + s) % nx) + c, v)
        wp_c.append(go(remote(wp.at[i], wp.at[i], wp_s.at[s - 1], wp_r.at[s - 1], dev)))
    wp_sib = [go(remote(wp.at[i], wp.at[i], wp_s.at[nx - 1], wp_r.at[nx - 1], (sib, v)))]

    rows = bufb.shape[0] * bufb.shape[1]
    r_io = lax.broadcasted_iota(jnp.int32, (rows, rows), 0)
    c_io = lax.broadcasted_iota(jnp.int32, (rows, rows), 1)
    src = ((r_io >> 2) & 7) * 32 + (r_io >> 5) * 4 + (r_io & 3)
    perm = jnp.where(src == c_io, 1.0, 0.0).astype(jnp.bfloat16)
    for cp in xd:
        cp.wait_recv()
    moved = jnp.dot(perm, bufb[...].reshape(rows, feat), preferred_element_type=jnp.float32)
    xp[...] = moved.astype(jnp.bfloat16).reshape(xp.shape)
    xz = []
    for s in range(1, nz):
        zt = (z + s) % nz
        xz.append(go(remote(xp.at[zt], bufx.at[z], xz_s.at[s - 1], xz_r.at[s - 1], (i, vz(s)))))
    bufx[z] = xp[z]

    def ring_step(s):
        if s <= n_right:
            rights[s - 1].wait_recv()
            origin = (z - s + nz) % nz
            if s < n_right:
                rights.append(go(ring_copy(origin, s + 1, 1)))
            sibs.append(go(sib_copy(origin, s - 1)))
        if s <= n_left:
            lefts[s - 1].wait_recv()
            origin = (z + s) % nz
            if s < n_left:
                lefts.append(go(ring_copy(origin, s + 1, -1)))
            sibs.append(go(sib_copy(origin, n_right + s - 1)))

    ring_step(1)
    for s in range(1, nx):
        we_c[s - 1].wait_recv()
        o = 2 * ((x - s + nx) % nx) + c
        we_sib.append(
            go(remote(we.at[o], we.at[o], we_s.at[nx - 1 + s], we_r.at[nx - 1 + s], (sib, v)))
        )
    ring_step(2)
    for cp in xz:
        cp.wait_recv()
    for cp in we_sib:
        cp.wait_recv()
    acc = jnp.dot(bufx[0], we[0], preferred_element_type=jnp.float32)
    for k in range(1, nz):
        acc = acc + jnp.dot(bufx[k], we[k], preferred_element_type=jnp.float32)
    part[y] = acc
    ys = []
    for s in range(1, NY):
        ys.append(go(remote(part.at[y], part.at[y], y_s.at[s - 1], y_r.at[s - 1], (i, vy(s)))))
    for s in range(1, nx):
        wp_c[s - 1].wait_recv()
        o = 2 * ((x - s + nx) % nx) + c
        wp_sib.append(
            go(remote(wp.at[o], wp.at[o], wp_s.at[nx - 1 + s], wp_r.at[nx - 1 + s], (sib, v)))
        )
    for s in range(3, max(n_right, n_left) + 1):
        ring_step(s)
    for cp in wp_sib:
        cp.wait_recv()
    prow_copy.wait()
    positions = prow.shape[0]
    pp = jnp.dot(prow[...], wp[...].reshape(-1, width), preferred_element_type=jnp.float32)
    pred[...] = jnp.zeros_like(pred)
    pred[0:positions, :] = pp.astype(jnp.bfloat16).astype(jnp.float32)
    for cp in ys:
        cp.wait_recv()
    total = part[0]
    for k in range(1, NY):
        total = total + part[k]
    enc[...] = total.astype(jnp.bfloat16).astype(jnp.float32)
    for cp in sibs:
        cp.wait_recv()

    nvoc = wt.shape[0] * wt.shape[1]
    block_cols = wt.shape[1]
    upad = wlab.shape[0] * 8
    n_lab = labels.shape[1]
    lab_rows = jnp.broadcast_to(labels[pl.ds(z, 1), :], (n_lab, n_lab)).astype(jnp.float32).T
    lab_rows = jnp.concatenate([lab_rows, jnp.zeros((upad - n_lab, n_lab), jnp.float32)], axis=0)
    lane = lax.broadcasted_iota(jnp.int32, (upad, n_lab), 1)
    lab_acc = jnp.zeros((upad, width), jnp.float32)
    for k in range(wt.shape[0]):
        gid = (lane + (k * NY + y) * block_cols).astype(jnp.float32)
        onehot = jnp.where(lab_rows == gid, 1.0, 0.0).astype(jnp.bfloat16)
        lab_acc = lab_acc + jnp.dot(onehot, wt[k], preferred_element_type=jnp.float32)
    wlab[...] = jnp.zeros_like(wlab)
    for k in range(wlab.shape[0]):
        wlab[k, 0:8, :] = lab_acc[8 * k : 8 * k + 8, :].astype(jnp.bfloat16)

    cells = 8 * frames
    sub_r = lax.broadcasted_iota(jnp.int32, (16, cells), 0)
    sub_l = lax.broadcasted_iota(jnp.int32, (16, cells), 1) // frames
    label_mask = sub_r == sub_l
    chunk = 2

    def block(g, k):
        kk = g * 8 + k
        ev = enc[...]
        for s in range(8):
            h = jnp.tanh(ev + pred[pl.ds(kk * 8 + s, 1), :])
            hid[s * frames : (s + 1) * frames, :] = h.astype(jnp.bfloat16)
        hv = hid[...]
        ms, ss = [], []
        blank = None
        for q in range(wt.shape[0] // chunk):
            w = wt[q * chunk : (q + 1) * chunk].reshape(chunk * block_cols, width)
            lg = lax.dot_general(w, hv, NT, preferred_element_type=jnp.float32)
            if q == 0:
                blank = lg[0:1, :]
            m = jnp.max(lg, axis=0, keepdims=True)
            ms.append(m)
            ss.append(jnp.sum(jnp.exp(lg - m), axis=0, keepdims=True))
        ll = lax.dot_general(wlab[kk], hv, NT, preferred_element_type=jnp.float32)
        lab = jnp.sum(jnp.where(label_mask, ll, 0.0), axis=0, keepdims=True)
        top = functools.reduce(jnp.maximum, ms)
        tot = functools.reduce(jnp.add, [a * jnp.exp(b - top) for a, b in zip(ss, ms)])
        stat[y, g, 0, pl.ds(k, 1), :] = top + jnp.log(tot)
        stat[y, g, 1, pl.ds(k, 1), :] = lab
        stat[y, g, 2, pl.ds(k, 1), :] = blank

    n_blocks = wlab.shape[0]
    sts = []
    for g in range(stat.shape[1]):
        lax.fori_loop(0, min(8, n_blocks - 8 * g), lambda k, u, g=g: (block(g, k), u)[1], 0)
        for s in range(1, NY):
            idx = g * (NY - 1) + s - 1
            sts.append(
                go(remote(stat.at[y, g], stat.at[y, g], st_s.at[idx], st_r.at[idx], (i, vy(s))))
            )
    for cp in sts:
        cp.wait_recv()

    for g in range(stat.shape[1]):
        lses = [stat[k, g, 0] for k in range(NY)]
        top = functools.reduce(jnp.maximum, lses)
        log_norm = top + jnp.log(functools.reduce(jnp.add, [jnp.exp(a - top) for a in lses]))
        label_lp = functools.reduce(jnp.add, [stat[k, g, 1] for k in range(NY)]) - log_norm
        blank_lp = stat[0, g, 2] - log_norm
        for a, val in enumerate((blank_lp, label_lp)):
            for s in range(8):
                h = val[:, 128 * (s // 4) : 128 * (s // 4) + 128]
                if s % 4:
                    h = pltpu.roll(h, 128 - 32 * (s % 4), 1)
                lp[a, pl.ds(64 * g + s, 8, stride=8), :] = h
    lanes = lax.broadcasted_iota(jnp.int32, lp.shape[1:], 1)
    for a in range(2):
        val = lp[a]
        for bit in range(5):
            val = jnp.where((lanes >> bit) & 1 == 1, pltpu.roll(val, 1 << bit, 0), val)
        lp[a] = val

    t_len = flen[z]
    u_len = llen[z]
    lane8 = lax.broadcasted_iota(jnp.int32, (8, 128), 1)
    first = lane8 == 0
    when = jnp.where(lane8 == t_len - 1, t_len - 1 + u_len, -1)

    def advance(d, state):
        e, m, res, resm = state
        b_d = jnp.broadcast_to(lp[0, pl.ds(d, 1), :], (8, 128))
        l_d = jnp.broadcast_to(lp[1, pl.ds(d, 1), :], (8, 128))
        ending = e + b_d
        hit = when == d
        res = jnp.where(hit, ending, res)
        resm = jnp.where(hit, m, resm)
        a = jnp.where(first, NEG, pltpu.roll(ending, 1, 1))
        cc = e + l_d
        e2 = jnp.maximum(a, cc)
        m2 = jnp.where(first, 0.0, pltpu.roll(m, 1, 1)) * jnp.exp(a - e2) + m * jnp.exp(cc - e2)
        return e2, m2, res, resm

    state0[0] = jnp.where(first, 0.0, NEG)
    state0[1] = jnp.where(first, 1.0, 0.0)
    state0[2] = jnp.zeros((8, 128), jnp.float32)
    state0[3] = jnp.ones((8, 128), jnp.float32)
    start = tuple(state0[k] for k in range(4))
    unused_e, unused_m, res, resm = lax.fori_loop(0, 160, advance, start, unroll=8)
    val = jnp.sum(res + jnp.log(resm), axis=1, keepdims=True)
    loss = -val / (t_len + u_len).astype(jnp.float32)
    lossbuf[z] = jnp.broadcast_to(loss, (8, 128))
    los = []
    for s in range(1, nz):
        los.append(
            go(remote(lossbuf.at[z], lossbuf.at[z], lo_s.at[s - 1], lo_r.at[s - 1], (i, vz(s))))
        )
    for cp in los:
        cp.wait_recv()
    for k in range(nz):
        out[k : k + 1, :] = lossbuf[k, 0:1, :]
    for cp in sends:
        cp.wait_send()


def shards(ndp, nv, encoder_rows, predictor_rows, enc_weight, pred_weight, out_weight, flen, llen, labels):
    utts, fr, feat = encoder_rows.shape
    nz = nv // NY
    per = predictor_rows.shape[0]
    positions = predictor_rows.shape[1]
    width = enc_weight.shape[1]
    frames = fr * ndp
    cols = out_weight.shape[1]
    n_blocks = (positions + 7) // 8
    groups = (n_blocks + 7) // 8
    xin = encoder_rows.reshape(ndp, per * fr, feat)
    vm = pl.BlockSpec(memory_space=pltpu.VMEM)
    sm = pl.BlockSpec(memory_space=pltpu.SMEM)
    dma = pltpu.SemaphoreType.DMA
    bf, f32 = jnp.bfloat16, jnp.float32
    nx = ndp // 2
    res = pl.pallas_call(
        functools.partial(joint_kernel, ndp, nv),
        out_shape=jax.ShapeDtypeStruct((per, 128), f32),
        in_specs=[vm, pl.BlockSpec(memory_space=pl.ANY), vm, vm, vm, sm, sm, vm],
        out_specs=vm,
        scratch_shapes=[
            pltpu.VMEM((ndp, per * fr, feat), bf),
            pltpu.VMEM((nz, frames, feat), bf),
            pltpu.VMEM((nz, frames, feat), bf),
            pltpu.VMEM((ndp, feat, width), bf),
            pltpu.VMEM((ndp, pred_weight.shape[0], width), bf),
            pltpu.VMEM((positions, predictor_rows.shape[2]), bf),
            pltpu.VMEM((NY, frames, width), f32),
            pltpu.VMEM((frames, width), f32),
            pltpu.VMEM((8 * n_blocks, width), f32),
            pltpu.VMEM((nz, cols, width), bf),
            pltpu.VMEM((n_blocks, 16, width), bf),
            pltpu.VMEM((8 * frames, width), bf),
            pltpu.VMEM((NY, groups, 3, 8, 8 * frames), f32),
            pltpu.VMEM((2, 64 * groups, 128), f32),
            pltpu.VMEM((nz, 8, 128), f32),
            pltpu.VMEM((4, 8, 128), f32),
            dma,
            dma((ndp - 1,)),
            dma((ndp - 1,)),
            dma((nz - 1,)),
            dma((nz - 1,)),
            dma((2 * nx - 1,)),
            dma((2 * nx - 1,)),
            dma((2 * nx - 1,)),
            dma((2 * nx - 1,)),
            dma((nz - 1,)),
            dma((nz - 1,)),
            dma((nz - 1,)),
            dma((nz - 1,)),
            dma((NY - 1,)),
            dma((NY - 1,)),
            dma((groups * (NY - 1),)),
            dma((groups * (NY - 1),)),
            dma((nz - 1,)),
            dma((nz - 1,)),
        ],
        compiler_params=pltpu.CompilerParams(
            collective_id=0, has_side_effects=True, vmem_limit_bytes=32 * 1024 * 1024
        ),
    )(xin, predictor_rows, enc_weight, pred_weight, out_weight, flen, llen, labels)
    return res[:, 0]


def solution(mesh):
    return jax.shard_map(
        functools.partial(shards, mesh.shape["dp"], mesh.shape["vocab"]),
        mesh=mesh,
        in_specs=(
            P(None, "dp", "vocab"),
            P("dp", None, None),
            P("dp", None),
            P("dp", None),
            P(None, "vocab"),
            P("dp"),
            P("dp"),
            P("dp", None),
        ),
        out_specs=P("dp"),
        check_vma=False,
    )
```

time: 1980 us -> 67.1 us (0.03)
  the two profiles are of different devices: /device:TPU:2 before, /device:TPU:1 now
where the time goes in v1:
time: 67.1 us; the launch traced here: 67 us
  Pallas kernels  63.7 us (95%)
  local copies, waits for them, and re-layouts  3.13 us (5%)
    pallas_call x1, Pallas kernels, shards(): pl.pallas_call(functools.partial(joint_kernel, ndp, nv), out_shape=jax.Sh...  63.7 us
    unnamed x14, local copies, waits for them, and re-layouts  2.5 us

profile of v1, /device:TPU:1, one launch (start us, length us, event | category | flops | bytes accessed | tf_op | source)
XLA Modules:
  0.0 67.0 jit_solution(9008521738047089045)
XLA Ops:
  0.0 0.0 copy-start.3
  0.0 0.0 copy-start.5
  0.0 0.0 copy-start.4
  0.0 0.0 copy-start.1
  0.0 0.0 copy-start.2
  0.0 0.0 copy-start
  0.0 1.0 %copy.11 = bf16[64,4,48]{2,1,0:T(4,128)(2,1)S(1)} copy(bf16[64,4,48]{0,2,1:T(8,128)(2,1)} %param.8) | data formatting | bytes 49152 | tf_op args[0]
  1.0 1.5 %copy.12.prows = bf16[8,129,640]{2,1,0:T(8,128)(2,1)S(1)} copy(bf16[8,129,640]{2,0,1:T(8,128)(2,1)} %param.9) | data formatting | bytes 2641920 | tf_op args[1]
  2.5 0.0 copy-done.3
  2.5 0.0 copy-done.5
  2.5 0.0 copy-done.4
  2.6 0.0 copy-done.1
  2.6 0.0 copy-done.2
  2.6 0.0 copy-done
  2.6 63.7 %shard_map.82 = f32[8,128]{1,0:T(8,128)S(1)} custom-call(bf16[8,32,48]{2,1,0:T(8,128)(2,1)S(1)} %bitcast.1, bf16[8,129,640]{2,1,0:T(8,128)(2,1)S(1)} %copy.12.prows, bf16[192,640]{1,0:T(8,128)(2,1)S(1)} %copy-done, bf16[80,640]{1,0:T(8,128)(2,1)S(1)} %copy-done.2, bf16[640,128]{1,0:T(8,128)(2,1)S(1)} %copy-done.1, s32[8]{0:T(128)S(1)} %copy-done.4, ...), custom_call_target="tpu_custom_call" | custom-call | tf_op jit(solution)/shard_map/pallas_call | solution.py:357
  66.3 0.6 slice_reduce_fusion
Async XLA Ops:
  0.0 2.5 %copy-start.3 = (s32[8,128]{1,0:T(8,128)S(1)}, s32[8,128]{1,0:T(8,128)}, u32[]{:S(2)}) copy-start(s32[8,128]{1,0:T(8,128)} %labels.1) | copy-start | bytes 12292
  0.0 2.5 %copy-start.5 = (s32[8]{0:T(128)S(1)}, s32[8]{0:T(128)}, u32[]{:S(2)}) copy-start(s32[8]{0:T(128)} %llen.1) | copy-start | bytes 100
  0.0 2.5 %copy-start.4 = (s32[8]{0:T(128)S(1)}, s32[8]{0:T(128)}, u32[]{:S(2)}) copy-start(s32[8]{0:T(128)} %flen.1) | copy-start | bytes 100
  0.0 2.5 %copy-start.1 = (bf16[640,128]{1,0:T(8,128)(2,1)S(1)}, bf16[640,128]{1,0:T(8,128)(2,1)}, u32[]{:S(2)}) copy-start(bf16[640,128]{1,0:T(8,128)(2,1)} %wout.1) | copy-start | bytes 491524
  0.0 2.5 %copy-start.2 = (bf16[80,640]{1,0:T(8,128)(2,1)S(1)}, bf16[80,640]{1,0:T(8,128)(2,1)}, u32[]{:S(2)}) copy-start(bf16[80,640]{1,0:T(8,128)(2,1)} %wpred.1) | copy-start | bytes 307204
  0.0 2.5 %copy-start = (bf16[192,640]{1,0:T(8,128)(2,1)S(1)}, bf16[192,640]{1,0:T(8,128)(2,1)}, u32[]{:S(2)}) copy-start(bf16[192,640]{1,0:T(8,128)(2,1)} %wenc.1) | copy-start | bytes 737284

commit v2 on v1

v2 whole, which is shorter than its diff:
```python
import functools

import jax
import jax.numpy as jnp
from jax import lax
from jax.experimental import pallas as pl
from jax.experimental.pallas import tpu as pltpu
from jax.sharding import PartitionSpec as P

MESH = pl.DeviceIdType.MESH
NY = 4
NEG = -1e30
CHUNK = 256
NT = (((1,), (1,)), ((), ()))


RELS = (0, 1, -1, 2, -2, 3, -3, 4)


def lse(terms):
    if len(terms) == 1:
        return terms[0]
    top = functools.reduce(jnp.maximum, terms)
    return top + jnp.log(tree(jnp.add, [jnp.exp(a - top) for a in terms]))


def tree(op, vals):
    vals = list(vals)
    while len(vals) > 1:
        vals = [op(vals[k], vals[k + 1]) if k + 1 < len(vals) else vals[k] for k in range(0, len(vals), 2)]
    return vals[0]


def compose(lo, hi):
    n = len(lo)
    moved = [[pltpu.roll(b, a, 1) if a else b for b in lo] for a in range(n)]
    return [
        lse([hi[a] + moved[a][j - a] for a in range(n) if 0 <= j - a < n]) for j in range(2 * n - 1)
    ]


def joint_kernel(
    ndp,
    nv,
    xt_h,
    prows_h,
    wenc_h,
    wpred_h,
    wout_h,
    flen_h,
    llen_h,
    labels_h,
    out,
    xt,
    prows,
    wout,
    labels,
    flen,
    llen,
    xin,
    bufb,
    xp,
    bufx,
    we,
    wp,
    part,
    enc,
    pred,
    wt,
    wlab,
    hid_a,
    hid_b,
    last_a,
    last_b,
    lg_a,
    lg_b,
    stat,
    lp,
    band2,
    band4,
    band8,
    lossbuf,
    state0,
    in_s,
    xd_s,
    xd_r,
    xz_s,
    xz_r,
    we_s,
    we_r,
    wp_s,
    wp_r,
    ring_s,
    ring_r,
    sib_s,
    sib_r,
    y_s,
    y_r,
    st_s,
    st_r,
    lo_s,
    lo_r,
):
    nz = nv // NY
    nx = ndp // 2
    i = lax.axis_index("dp")
    v = lax.axis_index("vocab")
    z = v // NY
    y = v % NY
    x = i // 2
    c = i % 2
    sib = 2 * x + (1 - c)
    frames = part.shape[1]
    width = part.shape[2]
    feat = we.shape[1]

    def vz(s):
        return ((z + s + nz) % nz) * NY + y

    def vy(s):
        return z * NY + (y + s) % NY

    barrier = pltpu.get_barrier_semaphore()
    for s in range(1, nz):
        pl.semaphore_signal(barrier, inc=1, device_id=(i, vz(s)), device_id_type=MESH)
    for s in range(1, ndp):
        pl.semaphore_signal(barrier, inc=1, device_id=((i + s) % ndp, v), device_id_type=MESH)
    for s in range(1, NY):
        pl.semaphore_signal(barrier, inc=1, device_id=(i, vy(s)), device_id_type=MESH)

    erow = pl.multiple_of(feat * y, 16)
    loads = []
    for k, (src, dst) in enumerate(
        (
            (xt_h, xt),
            (wout_h, wout),
            (wenc_h.at[pl.ds(erow, feat)], we.at[i]),
            (wpred_h, wp.at[i]),
            (prows_h, prows),
            (labels_h, labels),
            (flen_h, flen),
            (llen_h, llen),
        )
    ):
        cp = pltpu.make_async_copy(src, dst, in_s.at[k])
        cp.start()
        loads.append(cp)

    def remote(src, dst, ssem, rsem, dev):
        return pltpu.make_async_remote_copy(
            src_ref=src, dst_ref=dst, send_sem=ssem, recv_sem=rsem, device_id=dev, device_id_type=MESH
        )

    sends = []

    def go(cp):
        cp.start()
        sends.append(cp)
        return cp

    utts = xt.shape[1]
    fr = xt.shape[0] // feat
    mine = utts * fr
    r_io = lax.broadcasted_iota(jnp.int32, (mine, utts), 0)
    u_io = lax.broadcasted_iota(jnp.int32, (mine, utts), 1)
    loads[0].wait()
    moved = None
    for f in range(fr):
        pick = jnp.where(r_io == u_io * fr + f, 1.0, 0.0).astype(jnp.bfloat16)
        one = lax.dot_general(
            pick, xt[f * feat : (f + 1) * feat, :], NT, preferred_element_type=jnp.float32
        )
        moved = one if moved is None else moved + one
    xin[...] = moved.astype(jnp.bfloat16).reshape(xin.shape)
    bufb[i] = xin[i]
    block_cols = wout.shape[1]
    loads[1].wait()
    wt[0:block_cols, :] = wout[...].astype(jnp.float32).T.astype(jnp.bfloat16)
    stat[y, 2] = jnp.zeros(stat.shape[2:], jnp.float32)
    loads[2].wait()
    loads[3].wait()

    pl.semaphore_wait(barrier, (ndp - 1) + (nz - 1) + (NY - 1))

    xd = []
    for s in range(1, ndp):
        k = (i + s) % ndp
        xd.append(go(remote(xin.at[k], bufb.at[i], xd_s.at[s - 1], xd_r.at[s - 1], (k, v))))

    half = block_cols // 2

    def ring_slot(rel):
        pos = RELS.index(rel)
        return wt.at[pl.ds(pl.multiple_of(pos * block_cols + c * half, half), half)]

    n_right, n_left = nz // 2, nz - 1 - nz // 2

    def ring_copy(s, direction):
        def rel(k):
            if direction < 0:
                return k
            return nz // 2 if 2 * k == nz else -k

        idx = s - 1 if direction > 0 else n_right + s - 1
        return remote(
            ring_slot(rel(s - 1)), ring_slot(rel(s)), ring_s.at[idx], ring_r.at[idx], (i, vz(direction))
        )

    def sib_copy(rel, idx):
        blk = ring_slot(rel)
        return remote(blk, blk, sib_s.at[idx], sib_r.at[idx], (sib, v))

    rights = [go(ring_copy(1, 1))]
    lefts = [go(ring_copy(1, -1))]
    sibs = {}

    we_c, wp_c = [], []
    for s in range(1, nx):
        dev = (2 * ((x + s) % nx) + c, v)
        we_c.append(go(remote(we.at[i], we.at[i], we_s.at[s - 1], we_r.at[s - 1], dev)))
    we_sib = [go(remote(we.at[i], we.at[i], we_s.at[nx - 1], we_r.at[nx - 1], (sib, v)))]
    for s in range(1, nx):
        dev = (2 * ((x + s) % nx) + c, v)
        wp_c.append(go(remote(wp.at[i], wp.at[i], wp_s.at[s - 1], wp_r.at[s - 1], dev)))
    wp_sib = [go(remote(wp.at[i], wp.at[i], wp_s.at[nx - 1], wp_r.at[nx - 1], (sib, v)))]

    def ring_step(s):
        if s <= n_right:
            rights[s - 1].wait_recv()
            if s < n_right:
                rights.append(go(ring_copy(s + 1, 1)))
            rel = nz // 2 if 2 * s == nz else -s
            sibs[rel] = go(sib_copy(rel, s - 1))
        if s <= n_left:
            lefts[s - 1].wait_recv()
            if s < n_left:
                lefts.append(go(ring_copy(s + 1, -1)))
            sibs[s] = go(sib_copy(s, n_right + s - 1))

    rows = bufb.shape[0] * bufb.shape[1]
    r_io = lax.broadcasted_iota(jnp.int32, (rows, rows), 0)
    c_io = lax.broadcasted_iota(jnp.int32, (rows, rows), 1)
    src = ((r_io >> 2) & 7) * 32 + (r_io >> 5) * 4 + (r_io & 3)
    perm = jnp.where(src == c_io, 1.0, 0.0).astype(jnp.bfloat16)
    ring_step(1)
    for cp in xd:
        cp.wait_recv()
    moved = jnp.dot(perm, bufb[...].reshape(rows, feat), preferred_element_type=jnp.float32)
    xp[...] = moved.astype(jnp.bfloat16).reshape(xp.shape)
    xz = []
    for s in (4, 3, 5, 2, 6, 1, 7):
        zt = (z + s) % nz
        xz.append(go(remote(xp.at[zt], bufx.at[z], xz_s.at[s - 1], xz_r.at[s - 1], (i, vz(s)))))
    bufx[z] = xp[z]

    positions = prows.shape[0] // xin.shape[0]
    upad = pred.shape[0]
    loads[4].wait()
    p_r = lax.broadcasted_iota(jnp.int32, (upad, prows.shape[0]), 0)
    p_c = lax.broadcasted_iota(jnp.int32, (upad, prows.shape[0]), 1)
    pick = jnp.where(p_c == p_r * xin.shape[0] + z, 1.0, 0.0).astype(jnp.bfloat16)
    prow = jnp.dot(pick, prows[...], preferred_element_type=jnp.float32).astype(jnp.bfloat16)

    for s in range(1, nx):
        we_c[s - 1].wait_recv()
        o = 2 * ((x - s + nx) % nx) + c
        we_sib.append(
            go(remote(we.at[o], we.at[o], we_s.at[nx - 1 + s], we_r.at[nx - 1 + s], (sib, v)))
        )
    ring_step(2)
    for cp in xz:
        cp.wait_recv()
    for cp in we_sib:
        cp.wait_recv()
    part[y] = tree(
        jnp.add, [jnp.dot(bufx[k], we[k], preferred_element_type=jnp.float32) for k in range(nz)]
    )
    ys = []
    for s in (2, 1, 3):
        ys.append(go(remote(part.at[y], part.at[y], y_s.at[s - 1], y_r.at[s - 1], (i, vy(s)))))
    ring_step(3)
    for s in range(1, nx):
        wp_c[s - 1].wait_recv()
        o = 2 * ((x - s + nx) % nx) + c
        wp_sib.append(
            go(remote(wp.at[o], wp.at[o], wp_s.at[nx - 1 + s], wp_r.at[nx - 1 + s], (sib, v)))
        )
    for cp in wp_sib:
        cp.wait_recv()
    pp = jnp.dot(prow, wp[...].reshape(-1, width), preferred_element_type=jnp.float32)
    pred[...] = pp.astype(jnp.bfloat16).astype(jnp.float32)
    for rel in RELS[1:5]:
        sibs[rel].wait_recv()

    n_lab = labels.shape[1]
    loads[5].wait()
    lab_rows = jnp.broadcast_to(labels[pl.ds(z, 1), :], (n_lab, n_lab)).astype(jnp.float32).T
    lab_rows = jnp.concatenate([lab_rows, jnp.zeros((16, n_lab), jnp.float32)], axis=0)
    lane = lax.broadcasted_iota(jnp.int32, lab_rows.shape, 1)

    def label_part(p):
        zo = (z + RELS[p] + nz) % nz
        gid = (lane + (zo * NY + y) * block_cols).astype(jnp.float32)
        onehot = jnp.where(lab_rows == gid, 1.0, 0.0).astype(jnp.bfloat16)
        return jnp.dot(
            onehot, wt[p * block_cols : (p + 1) * block_cols, :], preferred_element_type=jnp.float32
        )

    lab_acc = [label_part(p) for p in range(5)]
    for cp in ys:
        cp.wait_recv()
    enc[...] = tree(jnp.add, [part[k] for k in range(NY)]).astype(jnp.bfloat16).astype(jnp.float32)

    cells = 8 * frames
    nvoc = nz * block_cols
    n_blocks = wlab.shape[0]

    def make_hidden(kk, dst):
        ev = enc[...]
        for s in range(8):
            h = jnp.tanh(ev + pred[pl.ds(kk * 8 + s, 1), :])
            dst[s * frames : (s + 1) * frames, :] = h.astype(jnp.bfloat16)

    make_hidden(0, hid_a)
    ring_step(4)
    for rel in RELS[5:]:
        sibs[rel].wait_recv()
    lab_acc = tree(jnp.add, lab_acc + [label_part(p) for p in range(5, nz)])
    blank_rows = lab_acc[n_lab + 8 : n_lab + 16, :]
    for k in range(n_blocks):
        both = jnp.concatenate([lab_acc[8 * k : 8 * k + 8, :], blank_rows], axis=0)
        wlab[k] = both.astype(jnp.bfloat16)
    tail_rows = last_a.shape[0] - 16
    head_rows = nvoc - tail_rows
    last_a[0:tail_rows, :] = wt[head_rows:nvoc, :]
    last_b[0:tail_rows, :] = wt[head_rows:nvoc, :]

    sub_r = lax.broadcasted_iota(jnp.int32, (16, cells), 0)
    sub_l = lax.broadcasted_iota(jnp.int32, (16, cells), 1) // frames
    label_mask = sub_r == sub_l

    def multiply(kk, src, last, dst):
        last[tail_rows:, :] = wlab[kk]
        hv = src[...]
        for q in range(0, head_rows, CHUNK):
            dst[q : q + CHUNK, :] = lax.dot_general(
                wt[q : q + CHUNK, :], hv, NT, preferred_element_type=jnp.float32
            )
        dst[head_rows:, :] = lax.dot_general(last[...], hv, NT, preferred_element_type=jnp.float32)

    def reduce_block(g, k, src):
        m = jnp.max(src[0:nvoc, :], axis=0, keepdims=True)
        t = jnp.sum(jnp.exp(src[0:nvoc, :] - m), axis=0, keepdims=True)
        ll = src[nvoc : nvoc + 16, :]
        stat[y, g, 0, pl.ds(k, 1), :] = m + jnp.log(t)
        stat[y, g, 1, pl.ds(k, 1), :] = jnp.sum(
            jnp.where(label_mask, ll, 0.0), axis=0, keepdims=True
        )
        stat[y, g, 2, pl.ds(k, 1), :] = ll[8:9, :]

    sts = []

    def send_stats(g):
        for s in (2, 1, 3):
            idx = g * (NY - 1) + s - 1
            sts.append(
                go(remote(stat.at[y, g], stat.at[y, g], st_s.at[idx], st_r.at[idx], (i, vy(s))))
            )

    make_hidden(1, hid_b)
    multiply(0, hid_a, last_a, lg_a)

    def two_blocks(j, unused, g):
        k = 2 * j
        make_hidden(k + 2, hid_a)
        multiply(k + 1, hid_b, last_b, lg_b)
        reduce_block(g, k - 8 * g, lg_a)
        make_hidden(k + 3, hid_b)
        multiply(k + 2, hid_a, last_a, lg_a)
        reduce_block(g, k + 1 - 8 * g, lg_b)
        return unused

    groups = stat.shape[1]
    for g in range(groups - 1):
        lax.fori_loop(4 * g, 4 * g + 4, functools.partial(two_blocks, g=g), 0)
        send_stats(g)
    reduce_block(groups - 1, 0, lg_a)
    send_stats(groups - 1)
    loads[6].wait()
    loads[7].wait()
    t_len = flen[z]
    u_len = llen[z]

    for cp in sts:
        cp.wait_recv()
    for g in range(stat.shape[1]):
        log_norm = lse([stat[k, g, 0] for k in range(NY)])
        label_lp = tree(jnp.add, [stat[k, g, 1] for k in range(NY)]) - log_norm
        blank_lp = stat[0, g, 2] - log_norm
        for a, val in enumerate((label_lp, blank_lp)):
            for s in range(8):
                h = val[:, 128 * (s // 4) : 128 * (s // 4) + 128]
                if s % 4:
                    h = pltpu.roll(h, 128 - 32 * (s % 4), 1)
                lp[a, pl.ds(64 * g + s, 8, stride=8), :] = h

    lanes = lax.broadcasted_iota(jnp.int32, lp.shape[1:], 1)
    upos = lax.broadcasted_iota(jnp.int32, lp.shape[1:], 0)
    label_lp = lp[0]
    blank_lp = lp[1]
    last = jnp.where((lanes == t_len - 1) & (upos == u_len), blank_lp, 0.0)
    last = jnp.sum(jnp.sum(last, axis=0, keepdims=True), axis=1, keepdims=True)
    label_lp = jnp.where((lanes == t_len - 1) & (upos >= u_len), 0.0, label_lp)
    blank_lp = jnp.where((lanes == t_len - 2) & (upos > u_len), NEG, blank_lp)
    for bit in range(5):
        moves = (lanes >> bit) & 1 == 1
        label_lp = jnp.where(moves, pltpu.roll(label_lp, 1 << bit, 0), label_lp)
        blank_lp = jnp.where(moves, pltpu.roll(blank_lp, 1 << bit, 0), blank_lp)
    lp[0] = label_lp
    lp[1] = jnp.where(lanes == 0, NEG, pltpu.roll(blank_lp, 1, 1))

    n = lp.shape[1]
    for src_ref, dst_ref in ((lp, band2), (band2, band4), (band4, band8)):
        n = n // 2
        lo = [src_ref[k, pl.ds(0, n, stride=2), :] for k in range(src_ref.shape[0])]
        hi = [src_ref[k, pl.ds(1, n, stride=2), :] for k in range(src_ref.shape[0])]
        for k, val in enumerate(compose(lo, hi)):
            dst_ref[k] = val

    lane8 = lax.broadcasted_iota(jnp.int32, (8, 128), 1)
    state0[0] = jnp.where(lane8 == 0, 0.0, NEG)
    state0[1] = jnp.ones((8, 128), jnp.float32)

    def advance(d, state):
        e, m = state
        nb = band8.shape[0]
        terms = [
            (pltpu.roll(e, j, 1) if j else e)
            + jnp.broadcast_to(band8[j, pl.ds(d, 1), :], (8, 128))
            for j in range(nb)
        ]
        top = tree(jnp.maximum, terms)
        m2 = tree(
            jnp.add,
            [(pltpu.roll(m, j, 1) if j else m) * jnp.exp(terms[j] - top) for j in range(nb)],
        )
        return top, m2

    e, m = lax.fori_loop(0, 20, advance, (state0[0], state0[1]), unroll=4)
    val = jnp.where(lane8 == t_len - 1, e + jnp.log(m), 0.0)
    val = jnp.sum(val, axis=1, keepdims=True) + last
    loss = -val / (t_len + u_len).astype(jnp.float32)
    lossbuf[z] = jnp.broadcast_to(loss, (8, 128))
    los = []
    for s in (4, 3, 5, 2, 6, 1, 7):
        los.append(
            go(remote(lossbuf.at[z], lossbuf.at[z], lo_s.at[s - 1], lo_r.at[s - 1], (i, vz(s))))
        )
    for cp in sends[: -len(los)]:
        cp.wait_send()
    for cp in los:
        cp.wait_recv()
    for k in range(nz):
        out[k : k + 1, :] = lossbuf[k, 0:1, :]
    for cp in los:
        cp.wait_send()


def shards(ndp, nv, encoder_rows, predictor_rows, enc_weight, pred_weight, out_weight, flen, llen, labels):
    utts, fr, feat = encoder_rows.shape
    nz = nv // NY
    per, positions, pwidth = predictor_rows.shape
    width = enc_weight.shape[1]
    frames = fr * ndp
    cols = out_weight.shape[1]
    n_blocks = (positions + 7) // 8
    groups = (n_blocks + 7) // 8
    cells = 8 * frames
    xt = jnp.transpose(encoder_rows, (1, 2, 0)).reshape(fr * feat, utts)
    prows = jnp.transpose(predictor_rows, (1, 0, 2)).reshape(positions * per, pwidth)
    vm = pl.BlockSpec(memory_space=pltpu.VMEM)
    hbm = pl.BlockSpec(memory_space=pltpu.HBM)
    dma = pltpu.SemaphoreType.DMA
    bf, f32, i32 = jnp.bfloat16, jnp.float32, jnp.int32
    nx = ndp // 2

    def pair(n):
        return [dma((n,)), dma((n,))]

    res = pl.pallas_call(
        functools.partial(joint_kernel, ndp, nv),
        out_shape=jax.ShapeDtypeStruct((per, 128), f32),
        in_specs=[hbm] * 8,
        out_specs=vm,
        scratch_shapes=[
            pltpu.VMEM(xt.shape, bf),
            pltpu.VMEM(prows.shape, bf),
            pltpu.VMEM(out_weight.shape, bf),
            pltpu.VMEM(labels.shape, i32),
            pltpu.SMEM(flen.shape, i32),
            pltpu.SMEM(llen.shape, i32),
            pltpu.VMEM((ndp, per * fr, feat), bf),
            pltpu.VMEM((ndp, per * fr, feat), bf),
            pltpu.VMEM((nz, frames, feat), bf),
            pltpu.VMEM((nz, frames, feat), bf),
            pltpu.VMEM((ndp, feat, width), bf),
            pltpu.VMEM((ndp, pred_weight.shape[0], width), bf),
            pltpu.VMEM((NY, frames, width), f32),
            pltpu.VMEM((frames, width), f32),
            pltpu.VMEM((8 * n_blocks + 8, width), f32),
            pltpu.VMEM((nz * cols, width), bf),
            pltpu.VMEM((n_blocks, 16, width), bf),
            pltpu.VMEM((cells, width), bf),
            pltpu.VMEM((cells, width), bf),
            pltpu.VMEM((CHUNK + 16, width), bf),
            pltpu.VMEM((CHUNK + 16, width), bf),
            pltpu.VMEM((nz * cols + 16, cells), f32),
            pltpu.VMEM((nz * cols + 16, cells), f32),
            pltpu.VMEM((NY, groups, 3, 8, cells), f32),
            pltpu.VMEM((2, 64 * groups, 128), f32),
            pltpu.VMEM((3, 32 * groups, 128), f32),
            pltpu.VMEM((5, 16 * groups, 128), f32),
            pltpu.VMEM((9, 8 * groups, 128), f32),
            pltpu.VMEM((nz, 8, 128), f32),
            pltpu.VMEM((2, 8, 128), f32),
            dma((8,)),
            *pair(ndp - 1),
            *pair(nz - 1),
            *pair(2 * nx - 1),
            *pair(2 * nx - 1),
            *pair(nz - 1),
            *pair(nz - 1),
            *pair(NY - 1),
            *pair(groups * (NY - 1)),
            *pair(nz - 1),
        ],
        compiler_params=pltpu.CompilerParams(
            collective_id=0, has_side_effects=True, vmem_limit_bytes=60 * 1024 * 1024
        ),
    )(xt, prows, enc_weight, pred_weight, out_weight, flen, llen, labels)
    return res[:, 0]


def solution(mesh):
    return jax.shard_map(
        functools.partial(shards, mesh.shape["dp"], mesh.shape["vocab"]),
        mesh=mesh,
        in_specs=(
            P(None, "dp", "vocab"),
            P("dp", None, None),
            P("dp", None),
            P("dp", None),
            P(None, "vocab"),
            P("dp"),
            P("dp"),
            P("dp", None),
        ),
        out_specs=P("dp"),
        check_vma=False,
    )
```

time: 67.1 us -> 49.7 us (0.74)
  Pallas kernels: 63.7 us -> 48.3 us
  local copies, waits for them, and re-layouts: 3.13 us -> 1.31 us
    pallas_call x1, Pallas kernels: 63.7 us -> 48.3 us  [shards(): pl.pallas_call(functools.partial(joint_kernel, ndp, nv), out_shape=jax.Sh...]
    unnamed x14 -> x0, local copies, waits for them, and re-layouts: 2.5 us -> none
    slice x1, local copies, waits for them, and re-layouts: 0.63 us -> 1.31 us  [shards(): return res[:, 0]]
where the time goes in v2:
time: 49.7 us; the launch traced here: 49.6 us
  Pallas kernels  48.3 us (97%)
  local copies, waits for them, and re-layouts  1.31 us (3%)
    pallas_call x1, Pallas kernels, shards(): pl.pallas_call(functools.partial(joint_kernel, ndp, nv), out_shape=jax.Sh...  48.3 us
    slice x1, local copies, waits for them, and re-layouts, shards(): return res[:, 0]  1.31 us

profile of v2, /device:TPU:1, one launch (start us, length us, event | category | flops | bytes accessed | tf_op | source)
XLA Modules:
  0.0 49.6 jit_solution(1517660893743534562)
XLA Ops:
  0.0 48.3 %shard_map.82 = f32[8,128]{1,0:T(8,128)} custom-call(bf16[192,64]{1,0:T(8,128)(2,1)} %bitcast.7, bf16[1032,640]{1,0:T(8,128)(2,1)} %bitcast.6, bf16[192,640]{1,0:T(8,128)(2,1)} %wenc_h.1, bf16[80,640]{1,0:T(8,128)(2,1)} %wpred_h.1, bf16[640,128]{1,0:T(8,128)(2,1)} %wout_h.1, s32[8]{0:T(128)} %flen_h.1, s32[8]{0:T(128)} %llen_h.1, s32[8,128]{1,0:T(8,128)} %labels_h.1), custom_call_target="tpu_custom_call" | custom-call | tf_op jit(solution)/shard_map/pallas_call | solution.py:490
  48.3 1.3 %slice_reduce_fusion = f32[8]{0:T(128)} fusion(f32[8,128]{1,0:T(8,128)} %shard_map.82), kind=kLoop, calls=%fused_computation | loop fusion | bytes 64 | tf_op jit(solution)/shard_map/slice | solution.py:541

commit v3 on v2

--- a/solution.py
+++ b/solution.py
@@ -10,6 +10,7 @@
 MESH = pl.DeviceIdType.MESH
 NY = 4
 NEG = -1e30
+FAR_FIRST = (4, 3, 5, 2, 6, 1, 7)
 CHUNK = 256
 NT = (((1,), (1,)), ((), ()))
 
@@ -72,9 +73,12 @@
     hid_b,
     last_a,
     last_b,
+    lab_near_s,
+    far_hot,
     lg_a,
     lg_b,
     stat,
+    stat2,
     lp,
     band2,
     band4,
@@ -121,7 +125,7 @@
         return z * NY + (y + s) % NY
 
     barrier = pltpu.get_barrier_semaphore()
-    for s in range(1, nz):
+    for s in FAR_FIRST:
         pl.semaphore_signal(barrier, inc=1, device_id=(i, vz(s)), device_id_type=MESH)
     for s in range(1, ndp):
         pl.semaphore_signal(barrier, inc=1, device_id=((i + s) % ndp, v), device_id_type=MESH)
@@ -176,7 +180,8 @@
     block_cols = wout.shape[1]
     loads[1].wait()
     wt[0:block_cols, :] = wout[...].astype(jnp.float32).T.astype(jnp.bfloat16)
-    stat[y, 2] = jnp.zeros(stat.shape[2:], jnp.float32)
+    stat[y, 1] = jnp.zeros(stat.shape[2:], jnp.float32)
+    stat2[y] = jnp.zeros(stat2.shape[1:], jnp.float32)
     loads[2].wait()
     loads[3].wait()
 
@@ -189,29 +194,24 @@
 
     half = block_cols // 2
 
-    def ring_slot(rel):
-        pos = RELS.index(rel)
-        return wt.at[pl.ds(pl.multiple_of(pos * block_cols + c * half, half), half)]
-
-    n_right, n_left = nz // 2, nz - 1 - nz // 2
-
-    def ring_copy(s, direction):
-        def rel(k):
-            if direction < 0:
-                return k
-            return nz // 2 if 2 * k == nz else -k
-
-        idx = s - 1 if direction > 0 else n_right + s - 1
+    def slot(rel, lo=0, n=half):
+        start = RELS.index(rel) * block_cols + c * half + lo
+        return wt.at[pl.ds(pl.multiple_of(start, 16), n)]
+
+    def ring_copy(rel, hop, idx, lo=0, n=half):
+        to = rel - hop
+        to = nz // 2 if abs(to) == nz // 2 else to
         return remote(
-            ring_slot(rel(s - 1)), ring_slot(rel(s)), ring_s.at[idx], ring_r.at[idx], (i, vz(direction))
-        )
-
-    def sib_copy(rel, idx):
-        blk = ring_slot(rel)
-        return remote(blk, blk, sib_s.at[idx], sib_r.at[idx], (sib, v))
-
-    rights = [go(ring_copy(1, 1))]
-    lefts = [go(ring_copy(1, -1))]
+            slot(rel, lo, n), slot(to, lo, n), ring_s.at[idx], ring_r.at[idx], (i, vz(hop))
+        )
+
+    def sib_copy(rel):
+        idx = RELS.index(rel) - 1
+        return remote(slot(rel), slot(rel), sib_s.at[idx], sib_r.at[idx], (sib, v))
+
+    ring = {}
+    for idx, hop in enumerate((1, -1, 2, -2)):
+        ring[-hop] = go(ring_copy(0, hop, idx))
     sibs = {}
 
     we_c, wp_c = [], []
@@ -224,34 +224,35 @@
         wp_c.append(go(remote(wp.at[i], wp.at[i], wp_s.at[s - 1], wp_r.at[s - 1], dev)))
     wp_sib = [go(remote(wp.at[i], wp.at[i], wp_s.at[nx - 1], wp_r.at[nx - 1], (sib, v)))]
 
-    def ring_step(s):
-        if s <= n_right:
-            rights[s - 1].wait_recv()
-            if s < n_right:
-                rights.append(go(ring_copy(s + 1, 1)))
-            rel = nz // 2 if 2 * s == nz else -s
-            sibs[rel] = go(sib_copy(rel, s - 1))
-        if s <= n_left:
-            lefts[s - 1].wait_recv()
-            if s < n_left:
-                lefts.append(go(ring_copy(s + 1, -1)))
-            sibs[s] = go(sib_copy(s, n_right + s - 1))
+    def to_sibling(*rels):
+        for rel in rels:
+            sibs[rel] = go(sib_copy(rel))
 
     rows = bufb.shape[0] * bufb.shape[1]
     r_io = lax.broadcasted_iota(jnp.int32, (rows, rows), 0)
     c_io = lax.broadcasted_iota(jnp.int32, (rows, rows), 1)
     src = ((r_io >> 2) & 7) * 32 + (r_io >> 5) * 4 + (r_io & 3)
     perm = jnp.where(src == c_io, 1.0, 0.0).astype(jnp.bfloat16)
-    ring_step(1)
+    for rel in (1, -1):
+        ring[rel].wait_recv()
+    to_sibling(1, -1)
     for cp in xd:
         cp.wait_recv()
     moved = jnp.dot(perm, bufb[...].reshape(rows, feat), preferred_element_type=jnp.float32)
     xp[...] = moved.astype(jnp.bfloat16).reshape(xp.shape)
     xz = []
-    for s in (4, 3, 5, 2, 6, 1, 7):
+    for s in FAR_FIRST:
         zt = (z + s) % nz
         xz.append(go(remote(xp.at[zt], bufx.at[z], xz_s.at[s - 1], xz_r.at[s - 1], (i, vz(s)))))
     bufx[z] = xp[z]
+
+    quarter = half // 2
+    for rel in (2, -2):
+        ring[rel].wait_recv()
+    ring[-3] = go(ring_copy(-2, 1, 4))
+    ring[3] = go(ring_copy(2, -1, 5))
+    fours = [go(ring_copy(-2, 2, 6, 0, quarter)), go(ring_copy(2, -2, 7, quarter, quarter))]
+    to_sibling(2, -2)
 
     positions = prows.shape[0] // xin.shape[0]
     upad = pred.shape[0]
@@ -267,18 +268,19 @@
         we_sib.append(
             go(remote(we.at[o], we.at[o], we_s.at[nx - 1 + s], we_r.at[nx - 1 + s], (sib, v)))
         )
-    ring_step(2)
     for cp in xz:
         cp.wait_recv()
     for cp in we_sib:
         cp.wait_recv()
     part[y] = tree(
         jnp.add, [jnp.dot(bufx[k], we[k], preferred_element_type=jnp.float32) for k in range(nz)]
-    )
+    ).astype(jnp.bfloat16)
     ys = []
     for s in (2, 1, 3):
         ys.append(go(remote(part.at[y], part.at[y], y_s.at[s - 1], y_r.at[s - 1], (i, vy(s)))))
-    ring_step(3)
+    for rel in (3, -3):
+        ring[rel].wait_recv()
+    to_sibling(3, -3)
     for s in range(1, nx):
         wp_c[s - 1].wait_recv()
         o = 2 * ((x - s + nx) % nx) + c
@@ -298,94 +300,117 @@
     lab_rows = jnp.concatenate([lab_rows, jnp.zeros((16, n_lab), jnp.float32)], axis=0)
     lane = lax.broadcasted_iota(jnp.int32, lab_rows.shape, 1)
 
-    def label_part(p):
+    def label_hot(p):
         zo = (z + RELS[p] + nz) % nz
         gid = (lane + (zo * NY + y) * block_cols).astype(jnp.float32)
-        onehot = jnp.where(lab_rows == gid, 1.0, 0.0).astype(jnp.bfloat16)
+        return jnp.where(lab_rows == gid, 1.0, 0.0).astype(jnp.bfloat16)
+
+    def label_part(p):
         return jnp.dot(
-            onehot, wt[p * block_cols : (p + 1) * block_cols, :], preferred_element_type=jnp.float32
-        )
-
-    lab_acc = [label_part(p) for p in range(5)]
+            label_hot(p),
+            wt[p * block_cols : (p + 1) * block_cols, :],
+            preferred_element_type=jnp.float32,
+        )
+
+    cells = 8 * frames
+    n_blocks = wlab.shape[0]
+    nvoc = nz * block_cols
+    near = 5
+    lab_near = tree(jnp.add, [label_part(p) for p in range(near)])
+    lab_near_s[...] = lab_near
+    far_hot[...] = jnp.concatenate([label_hot(p) for p in range(near, nz)], axis=1)
+    tail_rows = last_a.shape[0] - 16
+    last_a[0:tail_rows, :] = wt[0:tail_rows, :]
+    last_b[0:tail_rows, :] = wt[0:tail_rows, :]
+    for cp in fours:
+        cp.wait_recv()
+    to_sibling(4)
     for cp in ys:
         cp.wait_recv()
-    enc[...] = tree(jnp.add, [part[k] for k in range(NY)]).astype(jnp.bfloat16).astype(jnp.float32)
-
-    cells = 8 * frames
-    nvoc = nz * block_cols
-    n_blocks = wlab.shape[0]
-
-    def make_hidden(kk, dst):
+    enc[...] = tree(jnp.add, [part[k].astype(jnp.float32) for k in range(NY)]).astype(jnp.bfloat16).astype(jnp.float32)
+
+    def make_hidden(kk, dst, n=8):
         ev = enc[...]
-        for s in range(8):
+        for s in range(n):
             h = jnp.tanh(ev + pred[pl.ds(kk * 8 + s, 1), :])
             dst[s * frames : (s + 1) * frames, :] = h.astype(jnp.bfloat16)
 
+    def multiply(kk, src, last, dst, n=None, lo=None, hi=None):
+        n = n or cells
+        hv = src[0:n, :]
+        for q in range(lo or tail_rows, hi or nvoc, CHUNK):
+            dst[q : q + CHUNK, 0:n] = lax.dot_general(
+                wt[q : q + CHUNK, :], hv, NT, preferred_element_type=jnp.float32
+            )
+        if hi is None:
+            last[tail_rows:, :] = wlab[kk]
+            both = lax.dot_general(last[...], hv, NT, preferred_element_type=jnp.float32)
+            dst[0:tail_rows, 0:n] = both[0:tail_rows, :]
+            dst[nvoc:, 0:n] = both[tail_rows:, :]
+
     make_hidden(0, hid_a)
-    ring_step(4)
-    for rel in RELS[5:]:
+    make_hidden(1, hid_b)
+    multiply(0, hid_a, last_a, lg_a, hi=tail_rows + CHUNK)
+    for rel in RELS[near:]:
         sibs[rel].wait_recv()
-    lab_acc = tree(jnp.add, lab_acc + [label_part(p) for p in range(5, nz)])
+    lab_far = jnp.dot(
+        far_hot[...], wt[near * block_cols :, :], preferred_element_type=jnp.float32
+    )
+    lab_acc = lab_near_s[...] + lab_far
     blank_rows = lab_acc[n_lab + 8 : n_lab + 16, :]
     for k in range(n_blocks):
         both = jnp.concatenate([lab_acc[8 * k : 8 * k + 8, :], blank_rows], axis=0)
         wlab[k] = both.astype(jnp.bfloat16)
-    tail_rows = last_a.shape[0] - 16
-    head_rows = nvoc - tail_rows
-    last_a[0:tail_rows, :] = wt[head_rows:nvoc, :]
-    last_b[0:tail_rows, :] = wt[head_rows:nvoc, :]
 
     sub_r = lax.broadcasted_iota(jnp.int32, (16, cells), 0)
     sub_l = lax.broadcasted_iota(jnp.int32, (16, cells), 1) // frames
     label_mask = sub_r == sub_l
 
-    def multiply(kk, src, last, dst):
-        last[tail_rows:, :] = wlab[kk]
-        hv = src[...]
-        for q in range(0, head_rows, CHUNK):
-            dst[q : q + CHUNK, :] = lax.dot_general(
-                wt[q : q + CHUNK, :], hv, NT, preferred_element_type=jnp.float32
-            )
-        dst[head_rows:, :] = lax.dot_general(last[...], hv, NT, preferred_element_type=jnp.float32)
-
-    def reduce_block(g, k, src):
-        m = jnp.max(src[0:nvoc, :], axis=0, keepdims=True)
-        t = jnp.sum(jnp.exp(src[0:nvoc, :] - m), axis=0, keepdims=True)
-        ll = src[nvoc : nvoc + 16, :]
-        stat[y, g, 0, pl.ds(k, 1), :] = m + jnp.log(t)
-        stat[y, g, 1, pl.ds(k, 1), :] = jnp.sum(
-            jnp.where(label_mask, ll, 0.0), axis=0, keepdims=True
-        )
-        stat[y, g, 2, pl.ds(k, 1), :] = ll[8:9, :]
+    def reduce_block(src, n=None):
+        n = n or cells
+        m = jnp.max(src[0:nvoc, 0:n], axis=0, keepdims=True)
+        t = jnp.sum(jnp.exp(src[0:nvoc, 0:n] - m), axis=0, keepdims=True)
+        ll = src[nvoc : nvoc + 16, 0:n]
+        label = jnp.sum(jnp.where(label_mask[:, 0:n], ll, 0.0), axis=0, keepdims=True)
+        return m + jnp.log(t), label, ll[8:9, :]
+
+    def keep(g, k, src):
+        for a, val in enumerate(reduce_block(src)):
+            stat[y, g, a, pl.ds(k, 1), :] = val
 
     sts = []
 
-    def send_stats(g):
+    def send_stats(ref, g):
         for s in (2, 1, 3):
             idx = g * (NY - 1) + s - 1
-            sts.append(
-                go(remote(stat.at[y, g], stat.at[y, g], st_s.at[idx], st_r.at[idx], (i, vy(s))))
-            )
-
-    make_hidden(1, hid_b)
-    multiply(0, hid_a, last_a, lg_a)
+            sts.append(go(remote(ref, ref, st_s.at[idx], st_r.at[idx], (i, vy(s)))))
+
+    multiply(0, hid_a, last_a, lg_a, lo=tail_rows + CHUNK)
 
     def two_blocks(j, unused, g):
         k = 2 * j
         make_hidden(k + 2, hid_a)
         multiply(k + 1, hid_b, last_b, lg_b)
-        reduce_block(g, k - 8 * g, lg_a)
+        keep(g, k - 8 * g, lg_a)
         make_hidden(k + 3, hid_b)
         multiply(k + 2, hid_a, last_a, lg_a)
-        reduce_block(g, k + 1 - 8 * g, lg_b)
+        keep(g, k + 1 - 8 * g, lg_b)
         return unused
 
-    groups = stat.shape[1]
-    for g in range(groups - 1):
-        lax.fori_loop(4 * g, 4 * g + 4, functools.partial(two_blocks, g=g), 0)
-        send_stats(g)
-    reduce_block(groups - 1, 0, lg_a)
-    send_stats(groups - 1)
+    lax.fori_loop(0, 4, functools.partial(two_blocks, g=0), 0)
+    send_stats(stat.at[y, 0], 0)
+    lax.fori_loop(4, 7, functools.partial(two_blocks, g=1), 0)
+    lead = 128
+    make_hidden(n_blocks - 1, hid_a, lead // frames)
+    multiply(n_blocks - 2, hid_b, last_b, lg_b)
+    keep(1, n_blocks - 3 - 8, lg_a)
+    send_stats(stat.at[y, 1], 1)
+    multiply(n_blocks - 1, hid_a, last_a, lg_a, lead)
+    for a, val in enumerate(reduce_block(lg_b)):
+        stat2[y, 2 * a : 2 * a + 1, :] = val
+    for a, val in enumerate(reduce_block(lg_a, lead)):
+        stat2[y, 2 * a + 1 : 2 * a + 2, 0:lead] = val
+    send_stats(stat2.at[y], 2)
     loads[6].wait()
     loads[7].wait()
     t_len = flen[z]
@@ -393,10 +418,19 @@
 
     for cp in sts:
         cp.wait_recv()
-    for g in range(stat.shape[1]):
-        log_norm = lse([stat[k, g, 0] for k in range(NY)])
-        label_lp = tree(jnp.add, [stat[k, g, 1] for k in range(NY)]) - log_norm
-        blank_lp = stat[0, g, 2] - log_norm
+    row8 = lax.broadcasted_iota(jnp.int32, stat.shape[3:], 0)
+
+    def rows_of(k, g, a):
+        if g == 0:
+            return stat[k, 0, a]
+        if g == 1:
+            return jnp.where(row8 == 7, stat2[k, 2 * a : 2 * a + 1, :], stat[k, 1, a])
+        return jnp.where(row8 == 0, stat2[k, 2 * a + 1 : 2 * a + 2, :], 0.0)
+
+    for g in range(3):
+        log_norm = lse([rows_of(k, g, 0) for k in range(NY)])
+        label_lp = tree(jnp.add, [rows_of(k, g, 1) for k in range(NY)]) - log_norm
+        blank_lp = rows_of(0, g, 2) - log_norm
         for a, val in enumerate((label_lp, blank_lp)):
             for s in range(8):
                 h = val[:, 128 * (s // 4) : 128 * (s // 4) + 128]
@@ -452,7 +486,7 @@
     loss = -val / (t_len + u_len).astype(jnp.float32)
     lossbuf[z] = jnp.broadcast_to(loss, (8, 128))
     los = []
-    for s in (4, 3, 5, 2, 6, 1, 7):
+    for s in FAR_FIRST:
         los.append(
             go(remote(lossbuf.at[z], lossbuf.at[z], lo_s.at[s - 1], lo_r.at[s - 1], (i, vz(s))))
         )
@@ -505,7 +539,7 @@
             pltpu.VMEM((nz, frames, feat), bf),
             pltpu.VMEM((ndp, feat, width), bf),
             pltpu.VMEM((ndp, pred_weight.shape[0], width), bf),
-            pltpu.VMEM((NY, frames, width), f32),
+            pltpu.VMEM((NY, frames, width), bf),
             pltpu.VMEM((frames, width), f32),
             pltpu.VMEM((8 * n_blocks + 8, width), f32),
             pltpu.VMEM((nz * cols, width), bf),
@@ -514,9 +548,12 @@
             pltpu.VMEM((cells, width), bf),
             pltpu.VMEM((CHUNK + 16, width), bf),
             pltpu.VMEM((CHUNK + 16, width), bf),
+            pltpu.VMEM((labels.shape[1] + 16, width), f32),
+            pltpu.VMEM((labels.shape[1] + 16, (nz - 5) * cols), bf),
             pltpu.VMEM((nz * cols + 16, cells), f32),
             pltpu.VMEM((nz * cols + 16, cells), f32),
-            pltpu.VMEM((NY, groups, 3, 8, cells), f32),
+            pltpu.VMEM((NY, groups - 1, 3, 8, cells), f32),
+            pltpu.VMEM((NY, 8, cells), f32),
             pltpu.VMEM((2, 64 * groups, 128), f32),
             pltpu.VMEM((3, 32 * groups, 128), f32),
             pltpu.VMEM((5, 16 * groups, 128), f32),
@@ -528,7 +565,7 @@
             *pair(nz - 1),
             *pair(2 * nx - 1),
             *pair(2 * nx - 1),
-            *pair(nz - 1),
+            *pair(nz),
             *pair(nz - 1),
             *pair(NY - 1),
             *pair(groups * (NY - 1)),

time: 49.7 us -> 48.2 us (0.970)
  Pallas kernels: 48.3 us -> 46.5 us
    pallas_call x1, Pallas kernels: 48.3 us -> 46.5 us  [shards(): pl.pallas_call(functools.partial(joint_kernel, ndp, nv), out_shape=jax.Sh...]
where the time goes in v3:
time: 48.2 us; the launch traced here: 47.8 us
  Pallas kernels  46.5 us (96%)
  local copies, waits for them, and re-layouts  1.31 us (3%)
    pallas_call x1, Pallas kernels, shards(): pl.pallas_call(functools.partial(joint_kernel, ndp, nv), out_shape=jax.Sh...  46.5 us
    slice x1, local copies, waits for them, and re-layouts, shards(): return res[:, 0]  1.31 us

profile of v3, /device:TPU:1, one launch (start us, length us, event | category | flops | bytes accessed | tf_op | source)
XLA Modules:
  0.0 47.8 jit_solution(959425969285071917)
XLA Ops:
  0.0 46.5 %shard_map.82 = f32[8,128]{1,0:T(8,128)} custom-call(bf16[192,64]{1,0:T(8,128)(2,1)} %bitcast.7, bf16[1032,640]{1,0:T(8,128)(2,1)} %bitcast.6, bf16[192,640]{1,0:T(8,128)(2,1)} %wenc_h.1, bf16[80,640]{1,0:T(8,128)(2,1)} %wpred_h.1, bf16[640,128]{1,0:T(8,128)(2,1)} %wout_h.1, s32[8]{0:T(128)} %flen_h.1, s32[8]{0:T(128)} %llen_h.1, s32[8,128]{1,0:T(8,128)} %labels_h.1), custom_call_target="tpu_custom_call" | custom-call | tf_op jit(solution)/shard_map/pallas_call | solution.py:524
  46.5 1.3 %slice_reduce_fusion = f32[8]{0:T(128)} fusion(f32[8,128]{1,0:T(8,128)} %shard_map.82), kind=kLoop, calls=%fused_computation | loop fusion | bytes 64 | tf_op jit(solution)/shard_map/slice | solution.py:578

commit v4 on v3

--- a/solution.py
+++ b/solution.py
@@ -11,7 +11,7 @@
 NY = 4
 NEG = -1e30
 FAR_FIRST = (4, 3, 5, 2, 6, 1, 7)
-CHUNK = 256
+PRE = 6
 NT = (((1,), (1,)), ((), ()))
 
 
@@ -75,6 +75,8 @@
     last_b,
     lab_near_s,
     far_hot,
+    hid_pre,
+    lg_pre,
     lg_a,
     lg_b,
     stat,
@@ -319,9 +321,8 @@
     lab_near = tree(jnp.add, [label_part(p) for p in range(near)])
     lab_near_s[...] = lab_near
     far_hot[...] = jnp.concatenate([label_hot(p) for p in range(near, nz)], axis=1)
-    tail_rows = last_a.shape[0] - 16
-    last_a[0:tail_rows, :] = wt[0:tail_rows, :]
-    last_b[0:tail_rows, :] = wt[0:tail_rows, :]
+    near_rows = near * block_cols
+    far_rows = nvoc - near_rows
     for cp in fours:
         cp.wait_recv()
     to_sibling(4)
@@ -335,22 +336,30 @@
             h = jnp.tanh(ev + pred[pl.ds(kk * 8 + s, 1), :])
             dst[s * frames : (s + 1) * frames, :] = h.astype(jnp.bfloat16)
 
-    def multiply(kk, src, last, dst, n=None, lo=None, hi=None):
+    def multiply_near(src, dst, n=None):
         n = n or cells
         hv = src[0:n, :]
-        for q in range(lo or tail_rows, hi or nvoc, CHUNK):
-            dst[q : q + CHUNK, 0:n] = lax.dot_general(
-                wt[q : q + CHUNK, :], hv, NT, preferred_element_type=jnp.float32
+        first = 2 * block_cols
+        for lo, hi in ((0, first), (first, near_rows)):
+            dst[lo:hi, 0:n] = lax.dot_general(
+                wt[lo:hi, :], hv, NT, preferred_element_type=jnp.float32
             )
-        if hi is None:
-            last[tail_rows:, :] = wlab[kk]
-            both = lax.dot_general(last[...], hv, NT, preferred_element_type=jnp.float32)
-            dst[0:tail_rows, 0:n] = both[0:tail_rows, :]
-            dst[nvoc:, 0:n] = both[tail_rows:, :]
-
-    make_hidden(0, hid_a)
-    make_hidden(1, hid_b)
-    multiply(0, hid_a, last_a, lg_a, hi=tail_rows + CHUNK)
+
+    def multiply_far(kk, src, last, dst, n=None):
+        n = n or cells
+        last[far_rows:, :] = wlab[kk]
+        dst[near_rows:, 0:n] = lax.dot_general(
+            last[...], src[0:n, :], NT, preferred_element_type=jnp.float32
+        )
+
+    def multiply(kk, src, last, dst, n=None):
+        multiply_near(src, dst, n)
+        multiply_far(kk, src, last, dst, n)
+
+    for k in range(PRE):
+        make_hidden(k, hid_pre.at[k])
+        multiply_near(hid_pre.at[k], lg_pre.at[k])
+    make_hidden(PRE, hid_a)
     for rel in RELS[near:]:
         sibs[rel].wait_recv()
     lab_far = jnp.dot(
@@ -361,6 +370,8 @@
     for k in range(n_blocks):
         both = jnp.concatenate([lab_acc[8 * k : 8 * k + 8, :], blank_rows], axis=0)
         wlab[k] = both.astype(jnp.bfloat16)
+    last_a[0:far_rows, :] = wt[near_rows:, :]
+    last_b[0:far_rows, :] = wt[near_rows:, :]
 
     sub_r = lax.broadcasted_iota(jnp.int32, (16, cells), 0)
     sub_l = lax.broadcasted_iota(jnp.int32, (16, cells), 1) // frames
@@ -385,7 +396,13 @@
             idx = g * (NY - 1) + s - 1
             sts.append(go(remote(ref, ref, st_s.at[idx], st_r.at[idx], (i, vy(s)))))
 
-    multiply(0, hid_a, last_a, lg_a, lo=tail_rows + CHUNK)
+    for k in range(PRE):
+        multiply_far(k, hid_pre.at[k], last_b if k % 2 else last_a, lg_pre.at[k])
+        if k:
+            keep(0, k - 1, lg_pre.at[k - 1])
+    make_hidden(PRE + 1, hid_b)
+    multiply(PRE, hid_a, last_a, lg_a)
+    keep(0, PRE - 1, lg_pre.at[PRE - 1])
 
     def two_blocks(j, unused, g):
         k = 2 * j
@@ -397,7 +414,7 @@
         keep(g, k + 1 - 8 * g, lg_b)
         return unused
 
-    lax.fori_loop(0, 4, functools.partial(two_blocks, g=0), 0)
+    lax.fori_loop(PRE // 2, 4, functools.partial(two_blocks, g=0), 0)
     send_stats(stat.at[y, 0], 0)
     lax.fori_loop(4, 7, functools.partial(two_blocks, g=1), 0)
     lead = 128
@@ -546,10 +563,12 @@
             pltpu.VMEM((n_blocks, 16, width), bf),
             pltpu.VMEM((cells, width), bf),
             pltpu.VMEM((cells, width), bf),
-            pltpu.VMEM((CHUNK + 16, width), bf),
-            pltpu.VMEM((CHUNK + 16, width), bf),
+            pltpu.VMEM((3 * cols + 16, width), bf),
+            pltpu.VMEM((3 * cols + 16, width), bf),
             pltpu.VMEM((labels.shape[1] + 16, width), f32),
             pltpu.VMEM((labels.shape[1] + 16, (nz - 5) * cols), bf),
+            pltpu.VMEM((PRE, cells, width), bf),
+            pltpu.VMEM((PRE, nz * cols + 16, cells), f32),
             pltpu.VMEM((nz * cols + 16, cells), f32),
             pltpu.VMEM((nz * cols + 16, cells), f32),
             pltpu.VMEM((NY, groups - 1, 3, 8, cells), f32),

time: 48.2 us -> 47.1 us (0.977)
  Pallas kernels: 46.5 us -> 45.7 us
    pallas_call x1, Pallas kernels: 46.5 us -> 45.7 us  [shards(): pl.pallas_call(functools.partial(joint_kernel, ndp, nv), out_shape=jax.Sh...]
where the time goes in v4:
time: 47.1 us; the launch traced here: 47 us
  Pallas kernels  45.7 us (97%)
  local copies, waits for them, and re-layouts  1.31 us (3%)
    pallas_call x1, Pallas kernels, shards(): pl.pallas_call(functools.partial(joint_kernel, ndp, nv), out_shape=jax.Sh...  45.7 us
    slice x1, local copies, waits for them, and re-layouts, shards(): return res[:, 0]  1.31 us

profile of v4, /device:TPU:1, one launch (start us, length us, event | category | flops | bytes accessed | tf_op | source)
XLA Modules:
  0.0 47.0 jit_solution(49742971439713524)
XLA Ops:
  0.0 45.7 %shard_map.82 = f32[8,128]{1,0:T(8,128)} custom-call(bf16[192,64]{1,0:T(8,128)(2,1)} %bitcast.7, bf16[1032,640]{1,0:T(8,128)(2,1)} %bitcast.6, bf16[192,640]{1,0:T(8,128)(2,1)} %wenc_h.1, bf16[80,640]{1,0:T(8,128)(2,1)} %wpred_h.1, bf16[640,128]{1,0:T(8,128)(2,1)} %wout_h.1, s32[8]{0:T(128)} %flen_h.1, s32[8]{0:T(128)} %llen_h.1, s32[8,128]{1,0:T(8,128)} %labels_h.1), custom_call_target="tpu_custom_call" | custom-call | tf_op jit(solution)/shard_map/pallas_call | solution.py:541
  45.7 1.3 %slice_reduce_fusion = f32[8]{0:T(128)} fusion(f32[8,128]{1,0:T(8,128)} %shard_map.82), kind=kLoop, calls=%fused_computation | loop fusion | bytes 64 | tf_op jit(solution)/shard_map/slice | solution.py:597

commit v5 on v4

--- a/solution.py
+++ b/solution.py
@@ -11,7 +11,7 @@
 NY = 4
 NEG = -1e30
 FAR_FIRST = (4, 3, 5, 2, 6, 1, 7)
-PRE = 6
+PRE = 8
 NT = (((1,), (1,)), ((), ()))
 
 
@@ -340,7 +340,7 @@
         n = n or cells
         hv = src[0:n, :]
         first = 2 * block_cols
-        for lo, hi in ((0, first), (first, near_rows)):
+        for lo, hi in ((0, near_rows),):
             dst[lo:hi, 0:n] = lax.dot_general(
                 wt[lo:hi, :], hv, NT, preferred_element_type=jnp.float32
             )
@@ -416,7 +416,7 @@
 
     lax.fori_loop(PRE // 2, 4, functools.partial(two_blocks, g=0), 0)
     send_stats(stat.at[y, 0], 0)
-    lax.fori_loop(4, 7, functools.partial(two_blocks, g=1), 0)
+    lax.fori_loop(4, 7, functools.partial(two_blocks, g=1), 0, unroll=3)
     lead = 128
     make_hidden(n_blocks - 1, hid_a, lead // frames)
     multiply(n_blocks - 2, hid_b, last_b, lg_b)

time: 47.1 us -> 46.8 us (level)
  no operation moved by 1% of the time
where the time goes in v5:
time: 46.8 us; the launch traced here: 46.7 us
  Pallas kernels  45.4 us (97%)
  local copies, waits for them, and re-layouts  1.31 us (3%)
    pallas_call x1, Pallas kernels, shards(): pl.pallas_call(functools.partial(joint_kernel, ndp, nv), out_shape=jax.Sh...  45.4 us
    slice x1, local copies, waits for them, and re-layouts, shards(): return res[:, 0]  1.31 us

profile of v5, /device:TPU:1, one launch (start us, length us, event | category | flops | bytes accessed | tf_op | source)
XLA Modules:
  0.0 46.7 jit_solution(10595915110410309372)
XLA Ops:
  0.0 45.4 %shard_map.82 = f32[8,128]{1,0:T(8,128)} custom-call(bf16[192,64]{1,0:T(8,128)(2,1)} %bitcast.7, bf16[1032,640]{1,0:T(8,128)(2,1)} %bitcast.6, bf16[192,640]{1,0:T(8,128)(2,1)} %wenc_h.1, bf16[80,640]{1,0:T(8,128)(2,1)} %wpred_h.1, bf16[640,128]{1,0:T(8,128)(2,1)} %wout_h.1, s32[8]{0:T(128)} %flen_h.1, s32[8]{0:T(128)} %llen_h.1, s32[8,128]{1,0:T(8,128)} %labels_h.1), custom_call_target="tpu_custom_call" | custom-call | tf_op jit(solution)/shard_map/pallas_call | solution.py:541
  45.4 1.3 %slice_reduce_fusion = f32[8]{0:T(128)} fusion(f32[8,128]{1,0:T(8,128)} %shard_map.82), kind=kLoop, calls=%fused_computation | loop fusion | bytes 64 | tf_op jit(solution)/shard_map/slice | solution.py:597

commit v6 on v5

--- a/solution.py
+++ b/solution.py
@@ -12,6 +12,7 @@
 NEG = -1e30
 FAR_FIRST = (4, 3, 5, 2, 6, 1, 7)
 PRE = 8
+SPARE = 16
 NT = (((1,), (1,)), ((), ()))
 
 
@@ -143,7 +144,7 @@
             (wenc_h.at[pl.ds(erow, feat)], we.at[i]),
             (wpred_h, wp.at[i]),
             (prows_h, prows),
-            (labels_h, labels),
+            (labels_h, labels.at[pl.ds(0, labels_h.shape[0])]),
             (flen_h, flen),
             (llen_h, llen),
         )
@@ -455,10 +456,11 @@
                     h = pltpu.roll(h, 128 - 32 * (s % 4), 1)
                 lp[a, pl.ds(64 * g + s, 8, stride=8), :] = h
 
-    lanes = lax.broadcasted_iota(jnp.int32, lp.shape[1:], 1)
-    upos = lax.broadcasted_iota(jnp.int32, lp.shape[1:], 0)
-    label_lp = lp[0]
-    blank_lp = lp[1]
+    n = lp.shape[1] - SPARE
+    lanes = lax.broadcasted_iota(jnp.int32, (n, 128), 1)
+    upos = lax.broadcasted_iota(jnp.int32, (n, 128), 0)
+    label_lp = lp[0, 0:n, :]
+    blank_lp = lp[1, 0:n, :]
     last = jnp.where((lanes == t_len - 1) & (upos == u_len), blank_lp, 0.0)
     last = jnp.sum(jnp.sum(last, axis=0, keepdims=True), axis=1, keepdims=True)
     label_lp = jnp.where((lanes == t_len - 1) & (upos >= u_len), 0.0, label_lp)
@@ -467,16 +469,15 @@
         moves = (lanes >> bit) & 1 == 1
         label_lp = jnp.where(moves, pltpu.roll(label_lp, 1 << bit, 0), label_lp)
         blank_lp = jnp.where(moves, pltpu.roll(blank_lp, 1 << bit, 0), blank_lp)
-    lp[0] = label_lp
-    lp[1] = jnp.where(lanes == 0, NEG, pltpu.roll(blank_lp, 1, 1))
-
-    n = lp.shape[1]
+    lp[0, 0:n, :] = label_lp
+    lp[1, 0:n, :] = jnp.where(lanes == 0, NEG, pltpu.roll(blank_lp, 1, 1))
+
     for src_ref, dst_ref in ((lp, band2), (band2, band4), (band4, band8)):
         n = n // 2
         lo = [src_ref[k, pl.ds(0, n, stride=2), :] for k in range(src_ref.shape[0])]
         hi = [src_ref[k, pl.ds(1, n, stride=2), :] for k in range(src_ref.shape[0])]
         for k, val in enumerate(compose(lo, hi)):
-            dst_ref[k] = val
+            dst_ref[k, 0:n, :] = val
 
     lane8 = lax.broadcasted_iota(jnp.int32, (8, 128), 1)
     state0[0] = jnp.where(lane8 == 0, 0.0, NEG)
@@ -547,7 +548,7 @@
             pltpu.VMEM(xt.shape, bf),
             pltpu.VMEM(prows.shape, bf),
             pltpu.VMEM(out_weight.shape, bf),
-            pltpu.VMEM(labels.shape, i32),
+            pltpu.VMEM((2 * labels.shape[0], labels.shape[1]), i32),
             pltpu.SMEM(flen.shape, i32),
             pltpu.SMEM(llen.shape, i32),
             pltpu.VMEM((ndp, per * fr, feat), bf),
@@ -571,12 +572,12 @@
             pltpu.VMEM((PRE, nz * cols + 16, cells), f32),
             pltpu.VMEM((nz * cols + 16, cells), f32),
             pltpu.VMEM((nz * cols + 16, cells), f32),
-            pltpu.VMEM((NY, groups - 1, 3, 8, cells), f32),
+            pltpu.VMEM((NY + 1, groups - 1, 3, 8, cells), f32),
             pltpu.VMEM((NY, 8, cells), f32),
-            pltpu.VMEM((2, 64 * groups, 128), f32),
-            pltpu.VMEM((3, 32 * groups, 128), f32),
-            pltpu.VMEM((5, 16 * groups, 128), f32),
-            pltpu.VMEM((9, 8 * groups, 128), f32),
+            pltpu.VMEM((2, 64 * groups + SPARE, 128), f32),
+            pltpu.VMEM((3, 32 * groups + SPARE, 128), f32),
+            pltpu.VMEM((5, 16 * groups + SPARE, 128), f32),
+            pltpu.VMEM((9, 8 * groups + SPARE, 128), f32),
             pltpu.VMEM((nz, 8, 128), f32),
             pltpu.VMEM((2, 8, 128), f32),
             dma((8,)),

time: 46.8 us -> 46.8 us (level)
  no operation moved by 1% of the time
where the time goes in v6:
time: 46.8 us; the launch traced here: 46.7 us
  Pallas kernels  45.4 us (97%)
  local copies, waits for them, and re-layouts  1.31 us (3%)
    pallas_call x1, Pallas kernels, shards(): pl.pallas_call(functools.partial(joint_kernel, ndp, nv), out_shape=jax.Sh...  45.4 us
    slice x1, local copies, waits for them, and re-layouts, shards(): return res[:, 0]  1.31 us

profile of v6, /device:TPU:1, one launch (start us, length us, event | category | flops | bytes accessed | tf_op | source)
XLA Modules:
  0.0 46.7 jit_solution(16198531883031631224)
XLA Ops:
  0.0 45.4 %shard_map.82 = f32[8,128]{1,0:T(8,128)} custom-call(bf16[192,64]{1,0:T(8,128)(2,1)} %bitcast.7, bf16[1032,640]{1,0:T(8,128)(2,1)} %bitcast.6, bf16[192,640]{1,0:T(8,128)(2,1)} %wenc_h.1, bf16[80,640]{1,0:T(8,128)(2,1)} %wpred_h.1, bf16[640,128]{1,0:T(8,128)(2,1)} %wout_h.1, s32[8]{0:T(128)} %flen_h.1, s32[8]{0:T(128)} %llen_h.1, s32[8,128]{1,0:T(8,128)} %labels_h.1), custom_call_target="tpu_custom_call" | custom-call | tf_op jit(solution)/shard_map/pallas_call | solution.py:542
  45.4 1.3 %slice_reduce_fusion = f32[8]{0:T(128)} fusion(f32[8,128]{1,0:T(8,128)} %shard_map.82), kind=kLoop, calls=%fused_computation | loop fusion | bytes 64 | tf_op jit(solution)/shard_map/slice | solution.py:598

commit v7 on v6

--- a/solution.py
+++ b/solution.py
@@ -191,7 +191,7 @@
     pl.semaphore_wait(barrier, (ndp - 1) + (nz - 1) + (NY - 1))
 
     xd = []
-    for s in range(1, ndp):
+    for s in (4, 3, 5, 2, 6, 1, 7):
         k = (i + s) % ndp
         xd.append(go(remote(xin.at[k], bufb.at[i], xd_s.at[s - 1], xd_r.at[s - 1], (k, v))))
 
@@ -236,9 +236,6 @@
     c_io = lax.broadcasted_iota(jnp.int32, (rows, rows), 1)
     src = ((r_io >> 2) & 7) * 32 + (r_io >> 5) * 4 + (r_io & 3)
     perm = jnp.where(src == c_io, 1.0, 0.0).astype(jnp.bfloat16)
-    for rel in (1, -1):
-        ring[rel].wait_recv()
-    to_sibling(1, -1)
     for cp in xd:
         cp.wait_recv()
     moved = jnp.dot(perm, bufb[...].reshape(rows, feat), preferred_element_type=jnp.float32)
@@ -248,6 +245,9 @@
         zt = (z + s) % nz
         xz.append(go(remote(xp.at[zt], bufx.at[z], xz_s.at[s - 1], xz_r.at[s - 1], (i, vz(s)))))
     bufx[z] = xp[z]
+    for rel in (1, -1):
+        ring[rel].wait_recv()
+    to_sibling(1, -1)
 
     quarter = half // 2
     for rel in (2, -2):

time: 46.8 us -> 46.8 us (level)
  no operation moved by 1% of the time
where the time goes in v7:
time: 46.8 us; the launch traced here: 46.7 us
  Pallas kernels  45.3 us (97%)
  local copies, waits for them, and re-layouts  1.31 us (3%)
    pallas_call x1, Pallas kernels, shards(): pl.pallas_call(functools.partial(joint_kernel, ndp, nv), out_shape=jax.Sh...  45.3 us
    slice x1, local copies, waits for them, and re-layouts, shards(): return res[:, 0]  1.31 us

profile of v7, /device:TPU:1, one launch (start us, length us, event | category | flops | bytes accessed | tf_op | source)
XLA Modules:
  0.0 46.7 jit_solution(15607844985415515671)
XLA Ops:
  0.0 45.3 %shard_map.82 = f32[8,128]{1,0:T(8,128)} custom-call(bf16[192,64]{1,0:T(8,128)(2,1)} %bitcast.7, bf16[1032,640]{1,0:T(8,128)(2,1)} %bitcast.6, bf16[192,640]{1,0:T(8,128)(2,1)} %wenc_h.1, bf16[80,640]{1,0:T(8,128)(2,1)} %wpred_h.1, bf16[640,128]{1,0:T(8,128)(2,1)} %wout_h.1, s32[8]{0:T(128)} %flen_h.1, s32[8]{0:T(128)} %llen_h.1, s32[8,128]{1,0:T(8,128)} %labels_h.1), custom_call_target="tpu_custom_call" | custom-call | tf_op jit(solution)/shard_map/pallas_call | solution.py:542
  45.3 1.3 %slice_reduce_fusion = f32[8]{0:T(128)} fusion(f32[8,128]{1,0:T(8,128)} %shard_map.82), kind=kLoop, calls=%fused_computation | loop fusion | bytes 64 | tf_op jit(solution)/shard_map/slice | solution.py:598
